TPU v7x, 256 devices: a whole 4x4x8 slice. The times are simulated.
256 devices in a mesh: dp: 16 (over y_hi, x, core), mp: 16 (over z, y_lo).
Axes of the slice: x: 4, y: 4 (y_hi: 2, y_lo: 2; y = y_hi * 2 + y_lo), z: 8, core: 2. Of those that a mesh axis runs over, the one named last changes fastest.
Arguments:
- grid_fields: bfloat16 [16, 16384, 128], P('dp', 'mp'), may hold values from -2.09375 to 2.09375
- cotangent: bfloat16 [16, 2048, 1024], P('dp', 'mp'), may hold values from -6 to 6
- encoder_source: int32 [16, 2048], replicated, may hold values from 0 to 16383
- encoder_target: int32 [16, 2048], replicated, may hold values from 0 to 127
- encoder_count: int32 [16], replicated, may hold values from 512 to 2048, as said below
- mesh_source: int32 [16, 512], replicated, may hold values from 0 to 2047
- mesh_target: int32 [16, 512], replicated, may hold values from 0 to 127
- mesh_count: int32 [16], replicated, may hold values from 256 to 512, as said below
- w_encoder: bfloat16 [128, 1024], replicated, may hold values from -0.5 to 0.5
- w_query: bfloat16 [1024, 1024], replicated, may hold values from -0.1875 to 0.1875
- w_key: bfloat16 [1024, 1024], replicated, may hold values from -0.1875 to 0.1875
- w_value: bfloat16 [1024, 1024], replicated, may hold values from -0.1875 to 0.1875
- w_output: bfloat16 [1024, 1024], replicated, may hold values from -0.1875 to 0.1875
Outputs:
- grad_query: float32 [1024, 1024], P('mp')
- grad_key: float32 [1024, 1024], P('mp')
- grad_value: float32 [1024, 1024], P('mp')
- grad_output: float32 [1024, 1024], P('mp')
- grad_encoder: float32 [128, 1024], P('mp')
Inputs may be any that keep to these rules, and one draw needn't show every extreme that they name: `encoder_count`: live encoder slots of each block; a run of 1 neighbouring blocks is dense and one block is full. `mesh_count`: live processor slots of each block; one block is full.
All inputs are finite; a program needn't handle non-finite values.
Results may differ from a plain program's by a relative error of at most 0.014.
The roundings to bfloat16 on the way count: a program that leaves them out, or rounds other values in their place, can miss the bound.
Values may be sent and summed in bfloat16 or wider, within the bound.
No kernel may reach another device: no remote copies, remote signals or barrier semaphores. Data moves between devices by JAX's collectives and lax.ppermute only.
A program may use at most 128 MiB of HBM per device.

v0:
```python
import math

import jax
import jax.numpy as jnp
from jax import lax
from jax.sharding import PartitionSpec as P

BLOCK = 128
HD = 64


def widen(array):
    return array.astype(jnp.float32)


def times_transpose(left, weight):
    return lax.dot_general(
        left, weight, (((1,), (1,)), ((), ())), preferred_element_type=jnp.float32
    )


def column_terms(left, right):
    return lax.dot_general(
        left, right, (((0,), (0,)), ((), ())), preferred_element_type=jnp.float32
    )


def spread_sum(left, right):
    return lax.psum_scatter(column_terms(left, right), "mp", scatter_dimension=0, tiled=True)


def per_device(
    grid_fields,
    cotangent,
    encoder_source,
    encoder_target,
    encoder_count,
    mesh_source,
    mesh_target,
    mesh_count,
    w_encoder,
    w_query,
    w_key,
    w_value,
    w_output,
):
    model_size = lax.axis_size("mp")
    model_index = lax.axis_index("mp")
    local_grid = grid_fields[0]
    local_cot = cotangent[0]
    node_rows, width = local_cot.shape
    channels = local_grid.shape[1]
    all_nodes = node_rows * model_size
    own_blocks = node_rows // BLOCK
    enc_slots = encoder_source.shape[1]
    block_rows = lax.broadcasted_iota(jnp.int32, (BLOCK, 1), 0)
    first_block = model_index * own_blocks
    own_source = lax.dynamic_slice_in_dim(encoder_source, first_block, own_blocks, 0).reshape(-1)
    own_target = lax.dynamic_slice_in_dim(encoder_target, first_block, own_blocks, 0)
    own_count = lax.dynamic_slice_in_dim(encoder_count, first_block, own_blocks, 0)
    own_alive = (jnp.arange(enc_slots, dtype=jnp.int32)[None, :] < own_count[:, None]).reshape(-1)
    piece = lax.all_gather(local_grid, "mp", axis=0, tiled=True)
    inside = (own_source >= 0) & (own_source < piece.shape[0]) & own_alive
    fetched = jnp.take(piece, jnp.clip(own_source, 0, piece.shape[0] - 1), axis=0)
    slots = jnp.where(inside[:, None], fetched, jnp.zeros_like(fetched))
    selector = (own_target[:, None, :] == block_rows[None, :, :]).astype(jnp.bfloat16)
    encoded = jnp.einsum(
        "bne,bec->bnc",
        selector,
        slots.reshape(own_blocks, enc_slots, channels),
        preferred_element_type=jnp.float32,
    )
    encoded = encoded.reshape(node_rows, channels)
    encoded = encoded.astype(jnp.bfloat16)
    hidden = jnp.dot(encoded, w_encoder, preferred_element_type=jnp.float32).astype(jnp.bfloat16)
    query = jnp.dot(hidden, w_query, preferred_element_type=jnp.float32).astype(jnp.bfloat16)
    key_rows = jnp.dot(hidden, w_key, preferred_element_type=jnp.float32).astype(jnp.bfloat16)
    value = jnp.dot(hidden, w_value, preferred_element_type=jnp.float32).astype(jnp.bfloat16)
    grad_mixed = times_transpose(local_cot, w_output).astype(jnp.bfloat16)
    head_query, head_key, head_value, head_grad = (
        lax.all_to_all(query, "mp", split_axis=1, concat_axis=0, tiled=True),
        lax.all_to_all(key_rows, "mp", split_axis=1, concat_axis=0, tiled=True),
        lax.all_to_all(value, "mp", split_axis=1, concat_axis=0, tiled=True),
        lax.all_to_all(grad_mixed, "mp", split_axis=1, concat_axis=0, tiled=True),
    )
    head_width = head_query.shape[1]
    heads_here = head_width // HD
    blocks_all = mesh_source.shape[0]
    mesh_slots = mesh_source.shape[1]
    group_blocks = 4
    group_rows = group_blocks * BLOCK
    factor = 1.0 / math.sqrt(HD)

    def one_group(group_step, state):
        attended_all, grad_q_all, grad_k_sum, grad_v_sum = state
        first = group_step * group_blocks
        row_start = first * BLOCK
        sources = lax.dynamic_slice_in_dim(mesh_source, first, group_blocks, 0).reshape(-1)
        targets = lax.dynamic_slice_in_dim(mesh_target, first, group_blocks, 0)
        counts = lax.dynamic_slice_in_dim(mesh_count, first, group_blocks, 0)
        alive = (jnp.arange(mesh_slots, dtype=jnp.int32)[None, :] < counts[:, None]).reshape(-1)
        local_dest = (jnp.arange(group_blocks, dtype=jnp.int32)[:, None] * BLOCK + targets).reshape(
            -1
        )

        def rows_of(array):
            return lax.dynamic_slice_in_dim(array, row_start, group_rows, 0).reshape(
                group_rows, heads_here, HD
            )

        query_block = rows_of(head_query)
        key_block = rows_of(head_key)
        value_block = rows_of(head_value)
        grad_block = rows_of(head_grad)
        key_edge = jnp.take(head_key, sources, axis=0).reshape(-1, heads_here, HD)
        value_edge = jnp.take(head_value, sources, axis=0).reshape(-1, heads_here, HD)
        query_edge = jnp.take(query_block, local_dest, axis=0)
        grad_edge = jnp.take(grad_block, local_dest, axis=0)
        score = (
            jnp.einsum("ehd,ehd->eh", query_edge, key_edge, preferred_element_type=jnp.float32)
            * factor
        )
        expo = jnp.where(alive[:, None], jnp.exp(score), 0.0)
        self_expo = jnp.exp(
            jnp.einsum("nhd,nhd->nh", query_block, key_block, preferred_element_type=jnp.float32)
            * factor
        )
        total = jax.ops.segment_sum(expo, local_dest, num_segments=group_rows) + self_expo
        attn = expo / total[local_dest]
        attn_self = self_expo / total
        attn_round = attn.astype(jnp.bfloat16)
        self_round = attn_self.astype(jnp.bfloat16)
        attended = jax.ops.segment_sum(
            widen(attn_round)[:, :, None] * widen(value_edge), local_dest, num_segments=group_rows
        )
        attended = (attended + widen(self_round)[:, :, None] * widen(value_block)).astype(
            jnp.bfloat16
        )
        dattn = jnp.einsum("ehd,ehd->eh", grad_edge, value_edge, preferred_element_type=jnp.float32)
        dattn_self = jnp.einsum(
            "nhd,nhd->nh", grad_block, value_block, preferred_element_type=jnp.float32
        )
        mean_grad = (
            jax.ops.segment_sum(attn * dattn, local_dest, num_segments=group_rows)
            + attn_self * dattn_self
        )
        grad_score = (attn * (dattn - mean_grad[local_dest]) * factor).astype(jnp.bfloat16)
        grad_self = (attn_self * (dattn_self - mean_grad) * factor).astype(jnp.bfloat16)
        grad_q = jax.ops.segment_sum(
            widen(grad_score)[:, :, None] * widen(key_edge), local_dest, num_segments=group_rows
        )
        grad_q = (grad_q + widen(grad_self)[:, :, None] * widen(key_block)).astype(jnp.bfloat16)
        key_terms = (widen(grad_score)[:, :, None] * widen(query_edge)).reshape(-1, head_width)
        value_terms = (widen(attn_round)[:, :, None] * widen(grad_edge)).reshape(-1, head_width)
        grad_k_sum = grad_k_sum.at[sources].add(key_terms)
        grad_v_sum = grad_v_sum.at[sources].add(value_terms)
        key_self = (widen(grad_self)[:, :, None] * widen(query_block)).reshape(
            group_rows, head_width
        )
        value_self = (widen(self_round)[:, :, None] * widen(grad_block)).reshape(
            group_rows, head_width
        )
        grad_k_sum = lax.dynamic_update_slice_in_dim(
            grad_k_sum,
            lax.dynamic_slice_in_dim(grad_k_sum, row_start, group_rows, 0) + key_self,
            row_start,
            0,
        )
        grad_v_sum = lax.dynamic_update_slice_in_dim(
            grad_v_sum,
            lax.dynamic_slice_in_dim(grad_v_sum, row_start, group_rows, 0) + value_self,
            row_start,
            0,
        )
        attended_all = lax.dynamic_update_slice_in_dim(
            attended_all, attended.reshape(group_rows, head_width), row_start, 0
        )
        grad_q_all = lax.dynamic_update_slice_in_dim(
            grad_q_all, grad_q.reshape(group_rows, head_width), row_start, 0
        )
        return (attended_all, grad_q_all, grad_k_sum, grad_v_sum)

    start_state = (
        jnp.zeros((all_nodes, head_width), jnp.bfloat16),
        jnp.zeros((all_nodes, head_width), jnp.bfloat16),
        jnp.zeros((all_nodes, head_width), jnp.float32),
        jnp.zeros((all_nodes, head_width), jnp.float32),
    )
    attended_all, grad_q_all, grad_k_sum, grad_v_sum = lax.fori_loop(
        0, blocks_all // group_blocks, one_group, start_state
    )
    grad_k_all = grad_k_sum.astype(jnp.bfloat16)
    grad_v_all = grad_v_sum.astype(jnp.bfloat16)
    attended_n, grad_q_n, grad_k_n, grad_v_n = (
        lax.all_to_all(attended_all, "mp", split_axis=0, concat_axis=1, tiled=True),
        lax.all_to_all(grad_q_all, "mp", split_axis=0, concat_axis=1, tiled=True),
        lax.all_to_all(grad_k_all, "mp", split_axis=0, concat_axis=1, tiled=True),
        lax.all_to_all(grad_v_all, "mp", split_axis=0, concat_axis=1, tiled=True),
    )
    part_query = spread_sum(hidden, grad_q_n)
    part_key = spread_sum(hidden, grad_k_n)
    part_value = spread_sum(hidden, grad_v_n)
    norm = 1.0 / math.sqrt(lax.axis_size("dp") * all_nodes)
    part_output = spread_sum(attended_n, local_cot)
    grad_hidden = widen(local_cot) + times_transpose(grad_q_n, w_query)
    grad_hidden = grad_hidden + times_transpose(grad_k_n, w_key)
    grad_hidden = (grad_hidden + times_transpose(grad_v_n, w_value)).astype(jnp.bfloat16)
    part_encoder = spread_sum(encoded, grad_hidden)
    share_query, share_key, share_value, share_output, share_encoder = lax.psum(
        (part_query, part_key, part_value, part_output, part_encoder), "dp"
    )
    return (
        share_query * norm,
        share_key * norm,
        share_value * norm,
        share_output * norm,
        share_encoder * norm,
    )


def solution(mesh):
    in_specs = (
        P("dp", "mp", None),
        P("dp", "mp", None),
        P(),
        P(),
        P(),
        P(),
        P(),
        P(),
        P(),
        P(),
        P(),
        P(),
        P(),
    )
    out_specs = (P("mp", None), P("mp", None), P("mp", None), P("mp", None), P("mp", None))
    return jax.shard_map(
        per_device, mesh=mesh, in_specs=in_specs, out_specs=out_specs, check_vma=False
    )
```

profile of v0, /device:TPU:1, one launch (start us, length us, event | category | flops | bytes accessed | tf_op | source)
XLA Modules:
  0.0 1479.7 jit_solution(7634439328324552748)
XLA Ops:
  11.3 10.1 all-to-all-start.3
  25.3 88.4 %all-gather.3.cloned.1.call-done = bf16[1,16384,128]{2,1,0:T(8,128)(2,1)} async-done(((bf16[1,1024,128]{2,1,0:T(8,128)(2,1)}), bf16[1,16384,128]{2,1,0:T(8,128)(2,1)}) %all-gather.3.cloned.1.call-update) | async-done | bytes 4194320 | tf_op jit(solution)/shard_map/all_gather | solution.py:62
  113.7 8.4 gather_fusion.6
  159.9 7.2 all-to-all-done.2
  171.4 639.6 %while.21 = (s32[]{:T(128)}, bf16[2048,64]{1,0:T(8,128)(2,1)}, bf16[2048,64]{1,0:T(8,128)(2,1)}, f32[2048,64]{1,0:T(8,128)}, f32[2048,64]{1,0:T(8,128)}, /*index...) while((s32[]{:T(128)}, bf16[2048,64]{1,0:T(8,128)(2,1)}, ...), condition=%wide.region_7.10_spmd, body=%wide.region_0.9_spmd.sunk | while | flops 4346382 | bytes 9754503 | solution.py:189
  173.9 8.0 gather_fusion
  181.9 8.0 gather_fusion.1
  189.9 8.0 gather_fusion.2
  198.9 8.0 gather_fusion.3
  210.6 14.7 scatter_fusion
  225.4 13.2 gather_fusion.4
  238.6 15.5 %scatter_custom_fusion.25 = f32[2048,64]{1,0:T(8,128)} fusion(f32[2048,64]{1,0:T(8,128)} %get-tuple-element.497, s32[2048]{0:T(1024)S(1)} %bitcast.202, f32[2048]{0:T(1024)S(1)} %convert_convert_fusion.6, bf16[2048,64]{1,0:T(8,128)(2,1)} %gather_fusion, pred[2048]{0:T(1024)(128)(4,1)S(1)} %compare_and_fusion.5, bf16[]{:T(256)} %constant.125.clone.6..sunk), kind=kCustom, calls=%fused_computation.21.clone.1 | custom fusion | flops 524288 | bytes 1059328 | tf_op jit(solution)/shard_map/while/body/eval_jaxpr/scatter-add | solution.py:156
  256.0 14.7 scatter_fusion.1
  270.7 13.2 gather_fusion.5
  283.9 15.4 %scatter_custom_fusion.27 = f32[2048,64]{1,0:T(8,128)} fusion(f32[2048,64]{1,0:T(8,128)} %get-tuple-element.496, s32[2048]{0:T(1024)S(1)} %bitcast.203, f32[2048]{0:T(1024)S(1)} %fusion.95, bf16[2048,64]{1,0:T(8,128)(2,1)} %gather_fusion.3, pred[2048]{0:T(1024)(128)(4,1)S(1)} %compare_and_fusion.5, bf16[]{:T(256)} %constant.125.clone.6..sunk), kind=kCustom, calls=%fused_computation.23.clone.1 | custom fusion | flops 524288 | bytes 1059328 | tf_op jit(solution)/shard_map/while/body/eval_jaxpr/scatter-add | solution.py:155
  301.2 14.9 %scatter_custom_fusion.28 = f32[512,64]{1,0:T(8,128)} fusion(f32[512,64]{1,0:T(8,128)} %get-tuple-element.468, s32[2048]{0:T(1024)S(1)} %bitcast.171, f32[2048]{0:T(1024)S(1)} %fusion.95, bf16[2048,64]{1,0:T(8,128)(2,1)} %gather_fusion.2, pred[2048]{0:T(1024)(128)(4,1)S(1)} %compare_and_fusion.6, bf16[]{:T(256)} %constant.125.clone.6..sunk), kind=kCustom, calls=%fused_computation.20.clone.1 | custom fusion | flops 524288 | bytes 666112 | tf_op jit(solution)/shard_map/while/body/eval_jaxpr/scatter-add | solution.py:149
  316.1 13.4 scatter_custom_fusion.29
  333.8 8.0 gather_fusion
  341.8 8.0 gather_fusion.1
  349.8 8.0 gather_fusion.2
  358.8 8.0 gather_fusion.3
  370.5 14.7 scatter_fusion
  385.3 13.2 gather_fusion.4
  398.5 15.5 %scatter_custom_fusion.25 = f32[2048,64]{1,0:T(8,128)} fusion(f32[2048,64]{1,0:T(8,128)} %get-tuple-element.497, s32[2048]{0:T(1024)S(1)} %bitcast.202, f32[2048]{0:T(1024)S(1)} %convert_convert_fusion.6, bf16[2048,64]{1,0:T(8,128)(2,1)} %gather_fusion, pred[2048]{0:T(1024)(128)(4,1)S(1)} %compare_and_fusion.5, bf16[]{:T(256)} %constant.125.clone.6..sunk), kind=kCustom, calls=%fused_computation.21.clone.1 | custom fusion | flops 524288 | bytes 1059328 | tf_op jit(solution)/shard_map/while/body/eval_jaxpr/scatter-add | solution.py:156
  415.9 14.7 scatter_fusion.1
  430.6 13.2 gather_fusion.5
  443.8 15.4 %scatter_custom_fusion.27 = f32[2048,64]{1,0:T(8,128)} fusion(f32[2048,64]{1,0:T(8,128)} %get-tuple-element.496, s32[2048]{0:T(1024)S(1)} %bitcast.203, f32[2048]{0:T(1024)S(1)} %fusion.95, bf16[2048,64]{1,0:T(8,128)(2,1)} %gather_fusion.3, pred[2048]{0:T(1024)(128)(4,1)S(1)} %compare_and_fusion.5, bf16[]{:T(256)} %constant.125.clone.6..sunk), kind=kCustom, calls=%fused_computation.23.clone.1 | custom fusion | flops 524288 | bytes 1059328 | tf_op jit(solution)/shard_map/while/body/eval_jaxpr/scatter-add | solution.py:155
  461.1 14.9 %scatter_custom_fusion.28 = f32[512,64]{1,0:T(8,128)} fusion(f32[512,64]{1,0:T(8,128)} %get-tuple-element.468, s32[2048]{0:T(1024)S(1)} %bitcast.171, f32[2048]{0:T(1024)S(1)} %fusion.95, bf16[2048,64]{1,0:T(8,128)(2,1)} %gather_fusion.2, pred[2048]{0:T(1024)(128)(4,1)S(1)} %compare_and_fusion.6, bf16[]{:T(256)} %constant.125.clone.6..sunk), kind=kCustom, calls=%fused_computation.20.clone.1 | custom fusion | flops 524288 | bytes 666112 | tf_op jit(solution)/shard_map/while/body/eval_jaxpr/scatter-add | solution.py:149
  476.0 13.4 scatter_custom_fusion.29
  493.7 8.0 gather_fusion
  501.7 8.0 gather_fusion.1
  509.7 8.0 gather_fusion.2
  518.7 8.0 gather_fusion.3
  530.4 14.7 scatter_fusion
  545.2 13.2 gather_fusion.4
  558.4 15.5 %scatter_custom_fusion.25 = f32[2048,64]{1,0:T(8,128)} fusion(f32[2048,64]{1,0:T(8,128)} %get-tuple-element.497, s32[2048]{0:T(1024)S(1)} %bitcast.202, f32[2048]{0:T(1024)S(1)} %convert_convert_fusion.6, bf16[2048,64]{1,0:T(8,128)(2,1)} %gather_fusion, pred[2048]{0:T(1024)(128)(4,1)S(1)} %compare_and_fusion.5, bf16[]{:T(256)} %constant.125.clone.6..sunk), kind=kCustom, calls=%fused_computation.21.clone.1 | custom fusion | flops 524288 | bytes 1059328 | tf_op jit(solution)/shard_map/while/body/eval_jaxpr/scatter-add | solution.py:156
  575.8 14.7 scatter_fusion.1
  590.5 13.2 gather_fusion.5
  603.7 15.4 %scatter_custom_fusion.27 = f32[2048,64]{1,0:T(8,128)} fusion(f32[2048,64]{1,0:T(8,128)} %get-tuple-element.496, s32[2048]{0:T(1024)S(1)} %bitcast.203, f32[2048]{0:T(1024)S(1)} %fusion.95, bf16[2048,64]{1,0:T(8,128)(2,1)} %gather_fusion.3, pred[2048]{0:T(1024)(128)(4,1)S(1)} %compare_and_fusion.5, bf16[]{:T(256)} %constant.125.clone.6..sunk), kind=kCustom, calls=%fused_computation.23.clone.1 | custom fusion | flops 524288 | bytes 1059328 | tf_op jit(solution)/shard_map/while/body/eval_jaxpr/scatter-add | solution.py:155
  621.0 14.9 %scatter_custom_fusion.28 = f32[512,64]{1,0:T(8,128)} fusion(f32[512,64]{1,0:T(8,128)} %get-tuple-element.468, s32[2048]{0:T(1024)S(1)} %bitcast.171, f32[2048]{0:T(1024)S(1)} %fusion.95, bf16[2048,64]{1,0:T(8,128)(2,1)} %gather_fusion.2, pred[2048]{0:T(1024)(128)(4,1)S(1)} %compare_and_fusion.6, bf16[]{:T(256)} %constant.125.clone.6..sunk), kind=kCustom, calls=%fused_computation.20.clone.1 | custom fusion | flops 524288 | bytes 666112 | tf_op jit(solution)/shard_map/while/body/eval_jaxpr/scatter-add | solution.py:149
  635.9 13.4 scatter_custom_fusion.29
  653.5 8.0 gather_fusion
  661.6 8.0 gather_fusion.1
  669.6 8.0 gather_fusion.2
  678.6 8.0 gather_fusion.3
  690.3 14.7 scatter_fusion
  705.0 13.2 gather_fusion.4
  718.3 15.5 %scatter_custom_fusion.25 = f32[2048,64]{1,0:T(8,128)} fusion(f32[2048,64]{1,0:T(8,128)} %get-tuple-element.497, s32[2048]{0:T(1024)S(1)} %bitcast.202, f32[2048]{0:T(1024)S(1)} %convert_convert_fusion.6, bf16[2048,64]{1,0:T(8,128)(2,1)} %gather_fusion, pred[2048]{0:T(1024)(128)(4,1)S(1)} %compare_and_fusion.5, bf16[]{:T(256)} %constant.125.clone.6..sunk), kind=kCustom, calls=%fused_computation.21.clone.1 | custom fusion | flops 524288 | bytes 1059328 | tf_op jit(solution)/shard_map/while/body/eval_jaxpr/scatter-add | solution.py:156
  735.7 14.7 scatter_fusion.1
  750.4 13.2 gather_fusion.5
  763.6 15.4 %scatter_custom_fusion.27 = f32[2048,64]{1,0:T(8,128)} fusion(f32[2048,64]{1,0:T(8,128)} %get-tuple-element.496, s32[2048]{0:T(1024)S(1)} %bitcast.203, f32[2048]{0:T(1024)S(1)} %fusion.95, bf16[2048,64]{1,0:T(8,128)(2,1)} %gather_fusion.3, pred[2048]{0:T(1024)(128)(4,1)S(1)} %compare_and_fusion.5, bf16[]{:T(256)} %constant.125.clone.6..sunk), kind=kCustom, calls=%fused_computation.23.clone.1 | custom fusion | flops 524288 | bytes 1059328 | tf_op jit(solution)/shard_map/while/body/eval_jaxpr/scatter-add | solution.py:155
  780.9 14.9 %scatter_custom_fusion.28 = f32[512,64]{1,0:T(8,128)} fusion(f32[512,64]{1,0:T(8,128)} %get-tuple-element.468, s32[2048]{0:T(1024)S(1)} %bitcast.171, f32[2048]{0:T(1024)S(1)} %fusion.95, bf16[2048,64]{1,0:T(8,128)(2,1)} %gather_fusion.2, pred[2048]{0:T(1024)(128)(4,1)S(1)} %compare_and_fusion.6, bf16[]{:T(256)} %constant.125.clone.6..sunk), kind=kCustom, calls=%fused_computation.20.clone.1 | custom fusion | flops 524288 | bytes 666112 | tf_op jit(solution)/shard_map/while/body/eval_jaxpr/scatter-add | solution.py:149
  795.8 13.4 scatter_custom_fusion.29
  812.2 12.2 all_to_all.152
  832.1 12.2 all_to_all.153
  851.1 14.0 all_to_all.154
  869.1 14.9 %all_to_all.155 = bf16[16,128,64]{1,2,0:T(8,128)(2,1)S(1)} all-to-all(bf16[16,128,64]{1,2,0:T(8,128)(2,1)S(1)} %copy.65), channel_id=1, replica_groups=mesh['dp'=16,'mp'=16] {'mp'}, dimensions={0} | all-to-all | bytes 524288 | tf_op jit(solution)/shard_map/all_to_all | solution.py:195
  893.5 43.0 %reduce-scatter.6.cloned.1.call-done = f32[64,1024]{1,0:T(8,128)} async-done(((f32[1024,1024]{1,0:T(8,128)}), f32[64,1024]{1,0:T(8,128)}) %reduce-scatter.6.cloned.1.call-update) | async-done | bytes 262160 | tf_op jit(solution)/shard_map/reduce_scatter | solution.py:29
  936.4 103.0 %reduce-scatter.8.cloned.1.call-done = f32[64,1024]{1,0:T(8,128)} async-done(((f32[1024,1024]{1,0:T(8,128)}), f32[64,1024]{1,0:T(8,128)}) %reduce-scatter.8.cloned.1.call-update) | async-done | bytes 262160 | tf_op jit(solution)/shard_map/reduce_scatter | solution.py:29
  1039.4 101.9 %reduce-scatter.10.cloned.1.call-done = f32[64,1024]{1,0:T(8,128)} async-done(((f32[1024,1024]{1,0:T(8,128)}), f32[64,1024]{1,0:T(8,128)}) %reduce-scatter.10.cloned.1.call-update) | async-done | bytes 262160 | tf_op jit(solution)/shard_map/reduce_scatter | solution.py:29
  1141.3 102.4 %reduce-scatter.12.cloned.1.call-done = f32[64,1024]{1,0:T(8,128)} async-done(((f32[1024,1024]{1,0:T(8,128)}), f32[64,1024]{1,0:T(8,128)}) %reduce-scatter.12.cloned.1.call-update) | async-done | bytes 262160 | tf_op jit(solution)/shard_map/reduce_scatter | solution.py:29
  1243.8 63.6 %reduce-scatter.14.cloned.1.call-done = f32[8,1024]{1,0:T(8,128)} async-done(((f32[128,1024]{1,0:T(8,128)}), f32[8,1024]{1,0:T(8,128)}) %reduce-scatter.14.cloned.1.call-update) | async-done | bytes 32784 | tf_op jit(solution)/shard_map/reduce_scatter | solution.py:29
  1307.3 71.8 %psum.39 = f32[8,1024]{1,0:T(8,128)S(1)} all-reduce(f32[8,1024]{1,0:T(8,128)} %reduce-scatter.14.cloned.1.call-done), channel_id=1, replica_groups=mesh['dp'=16,'mp'=16] {'dp'}, use_global_device_ids=true, to_apply=%region_17.20 | all-reduce | flops 8192 | bytes 65536 | tf_op jit(solution)/shard_map/psum | solution.py:209
  1379.8 86.4 %all-reduce.3.cloned.1.call-done = (f32[64,1024]{1,0:T(8,128)}, f32[64,1024]{1,0:T(8,128)}, f32[64,1024]{1,0:T(8,128)}, f32[64,1024]{1,0:T(8,128)}) async-done(((f32[64,1024]{1,0:T(8,128)}, f32[64,1024]{1,0:T(8,128)}, f32[64,1024]{1,0:T(8,128)}, f32[64,1024]{1,0:T(8,128)}), (f32[64,1024]{1,0:T(8,128)}, f32[64,1024]{1,0:T(8,128)}, f32[64,1024]{1,0:T(8,128)}, ...) | async-done | bytes 1048592 | tf_op jit(solution)/shard_map/psum | solution.py:209
  (224 shorter events, 136.9 us)
Async XLA Ops:
  7.2 116.0 %copy-start = (bf16[1024,1024]{1,0:T(8,128)(2,1)S(1)}, bf16[1024,1024]{1,0:T(8,128)(2,1)}, u32[]{:S(2)}) copy-start(bf16[1024,1024]{1,0:T(8,128)(2,1)} %param.28) | copy-start | bytes 6291460
  7.2 14.3 copy-start.13
  7.2 106.5 %all-gather.3.cloned.1.call-start = ((), (), s32[]{:S(2)}) async-start(), calls=%async_computation.18 | async-start | bytes 4456448 | tf_op jit(solution)/shard_map/all_gather | solution.py:62
  11.3 113.2 %all-to-all-start.3 = ((bf16[128,16,64]{0,2,1:T(8,128)(2,1)}), bf16[128,16,64]{0,2,1:T(8,128)(2,1)S(1)}, u32[]{:S(2)}, u32[]{:S(2)}) async-start(bf16[128,16,64]{0,2,1:T(8,128)(2,1)} %bitcast.32), calls=%async_computation.3 | async-start | bytes 524288 | tf_op jit(solution)/shard_map/all_to_all | solution.py:84
  113.7 9.2 copy-start.12
  123.2 21.2 %copy-start.1 = (bf16[128,1024]{1,0:T(8,128)(2,1)}, bf16[128,1024]{1,0:T(8,128)(2,1)S(1)}, u32[]{:S(2)}) copy-start(bf16[128,1024]{1,0:T(8,128)(2,1)S(1)} %convolution_convert_fusion.4) | copy-start | bytes 786436
  124.5 16.4 %all-to-all-start = ((bf16[128,16,64]{0,2,1:T(8,128)(2,1)}), bf16[128,16,64]{0,2,1:T(8,128)(2,1)S(1)}, u32[]{:S(2)}, u32[]{:S(2)}) async-start(bf16[128,16,64]{0,2,1:T(8,128)(2,1)} %bitcast.22), calls=%async_computation | async-start | bytes 524288 | tf_op jit(solution)/shard_map/all_to_all | solution.py:81
  140.8 13.2 all-to-all-start.1
  154.0 13.1 all-to-all-start.2
  157.5 778.9 %reduce-scatter.6.cloned.1.call-start = ((), (), s32[]{:S(2)}) async-start(), calls=%async_computation.13 | async-start | bytes 4456448 | tf_op jit(solution)/shard_map/reduce_scatter | solution.py:29
  159.9 11.4 copy-start.14
  824.4 0.7 copy-start.7
  828.7 1.2 copy-start.3
  828.8 16.2 %copy-start.2 = (bf16[128,1024]{1,0:T(8,128)(2,1)S(1)}, bf16[128,1024]{1,0:T(8,128)(2,1)}, u32[]{:S(2)}) copy-start(bf16[128,1024]{1,0:T(8,128)(2,1)} %copy-done.1) | copy-start | bytes 786436
  828.8 210.7 %reduce-scatter.8.cloned.1.call-start = ((), (), s32[]{:S(2)}) async-start(), calls=%async_computation.14 | async-start | bytes 4456448 | tf_op jit(solution)/shard_map/reduce_scatter | solution.py:29
  844.3 0.7 copy-start.9
  847.7 1.2 copy-start.4
  847.7 293.6 %reduce-scatter.10.cloned.1.call-start = ((), (), s32[]{:S(2)}) async-start(), calls=%async_computation.15 | async-start | bytes 4456448 | tf_op jit(solution)/shard_map/reduce_scatter | solution.py:29
  867.8 1.0 copy-start.11
  867.8 16.1 %copy-start.6 = (bf16[1,128,1024]{2,1,0:T(8,128)(2,1)S(1)}, bf16[1,128,1024]{2,1,0:T(8,128)(2,1)}, u32[]{:S(2)}) copy-start(bf16[1,128,1024]{2,1,0:T(8,128)(2,1)} %param.20) | copy-start | bytes 786436
  867.8 375.9 %reduce-scatter.12.cloned.1.call-start = ((), (), s32[]{:S(2)}) async-start(), calls=%async_computation.16 | async-start | bytes 4456448 | tf_op jit(solution)/shard_map/reduce_scatter | solution.py:29
  886.6 1.0 copy-start.8
  886.6 1.8 copy-start.10
  886.6 420.7 %reduce-scatter.14.cloned.1.call-start = ((), (), s32[]{:S(2)}) async-start(), calls=%async_computation.17 | async-start | bytes 557056 | tf_op jit(solution)/shard_map/reduce_scatter | solution.py:29
  887.5 1.6 copy-start.5
  893.4 572.7 %all-reduce.3.cloned.1.call-start = ((), (), s32[]{:S(2)}) async-start(), calls=%async_computation.19 | async-start | bytes 2097152 | tf_op jit(solution)/shard_map/psum | solution.py:209
Sparse Core Ops, SparseCore 0:
  9.8 103.8 all-gather.2
  828.9 107.5 reduce-scatter.5
  939.0 100.3 reduce-scatter.7
  1041.8 99.4 reduce-scatter.9
  1143.7 100.0 reduce-scatter.11
  1246.1 61.2 reduce-scatter.13
  1310.5 155.6 all-reduce.2
where the time goes:
time: 1480 us
  waiting for transfers between devices  610 us (41%)
  other arithmetic  406 us (27%)
  local copies, waits for them, and re-layouts  275 us (19%)
  blocking collectives  125 us (8%)
  matrix products  24.8 us (2%)
  starting transfers between devices  24.2 us (2%)
    reduce_scatter x5, waiting for transfers between devices, spread_sum(): lax.psum_scatter(column_terms(left, right), 'mp', scatter_dimension=0, ti...  414 us
    all_gather x1, waiting for transfers between devices, per_device(): piece = lax.all_gather(local_grid, 'mp', axis=0, tiled=True)  88.4 us
    psum x1, waiting for transfers between devices, per_device(): lax.psum((part_query, part_key, part_value, part_output, part_encoder), '...  86.4 us
    psum x1, blocking collectives, per_device(): lax.psum((part_query, part_key, part_value, part_output, part_encoder), '...  71.8 us
    scatter-add x4, other arithmetic, one_group(): grad_v_sum = grad_v_sum.at[sources].add(value_terms)  62.1 us
    scatter-add x4, other arithmetic, one_group(): grad_k_sum = grad_k_sum.at[sources].add(key_terms)  61.8 us
    scatter-add x4, other arithmetic, one_group(): jax.ops.segment_sum(widen(grad_score)[:, :, None] * widen(key_edge), loca...  59.5 us
    scatter-add x4, other arithmetic, one_group(): jax.ops.segment_sum(expo, local_dest, num_segments=group_rows) + self_expo  58.7 us
  transfers between devices with their start and end apart: 11, of which 10 were waited for; matrix products, arithmetic and copies ran while one was open for 3% of the time, Pallas kernels for 0%

commit v1 on v0

v1 whole, which is shorter than its diff:
```python
import functools
import math

import jax
import jax.numpy as jnp
from jax import lax
from jax.experimental import pallas as pl
from jax.experimental.pallas import tpu as pltpu
from jax.sharding import PartitionSpec as P

BLOCK = 128
HD = 64
SLOT_CHUNK = 512
DEST_TILE = 256
ROW_CHUNK = 256
VMEM_LIMIT = 48 * 1024 * 1024


def dot_nn(left, right):
    return lax.dot_general(left, right, (((1,), (0,)), ((), ())), preferred_element_type=jnp.float32)


def dot_nt(left, right):
    return lax.dot_general(left, right, (((1,), (1,)), ((), ())), preferred_element_type=jnp.float32)


def dot_tn(left, right):
    return lax.dot_general(left, right, (((0,), (0,)), ((), ())), preferred_element_type=jnp.float32)


def encoder_kernel(
    count_ref, base_ref, source_ref, target_ref, grid_ref, w_output_ref, cot_ref, out_ref, pairs_ref
):
    block = pl.program_id(0)
    points = grid_ref.shape[0]
    slots = source_ref.shape[2]
    chunk = min(SLOT_CHUNK, slots)
    live = count_ref[block]
    base = base_ref[0]
    out_ref[0, BLOCK:, :] = dot_nt(w_output_ref[...], cot_ref[...]).astype(jnp.bfloat16)
    pairs_ref[...] = jnp.zeros_like(pairs_ref)

    def one_chunk(step, carry):
        first = pl.multiple_of(step * chunk, chunk)
        source = source_ref[0, :, pl.ds(first, chunk)] - base
        target = target_ref[0, :, pl.ds(first, chunk)]
        slot = first + lax.broadcasted_iota(jnp.int32, (1, chunk), 1)
        target = jnp.where(slot < live, target, -1)
        point_rows = lax.broadcasted_iota(jnp.int32, (points, chunk), 0)
        from_point = jnp.where(point_rows == source, 1.0, 0.0).astype(jnp.bfloat16)
        node_rows = lax.broadcasted_iota(jnp.int32, (BLOCK, chunk), 0)
        to_node = jnp.where(node_rows == target, 1.0, 0.0).astype(jnp.bfloat16)
        pairs_ref[...] += dot_nt(from_point, to_node)
        return carry

    lax.fori_loop(0, (live + chunk - 1) // chunk, one_chunk, 0)
    counts = pairs_ref[...].T.astype(jnp.bfloat16)
    out_ref[0, :BLOCK, :] = dot_nn(counts, grid_ref[...]).astype(jnp.bfloat16)


def encoder_partials(local_grid, source, target, count, base, w_output, local_cot):
    blocks, slots = source.shape
    points, channels = local_grid.shape
    node_rows, width = local_cot.shape
    head_rows = width // blocks
    return pl.pallas_call(
        encoder_kernel,
        grid_spec=pltpu.PrefetchScalarGridSpec(
            num_scalar_prefetch=2,
            grid=(blocks,),
            in_specs=[
                pl.BlockSpec((1, 1, slots), lambda b, *_: (b, 0, 0)),
                pl.BlockSpec((1, 1, slots), lambda b, *_: (b, 0, 0)),
                pl.BlockSpec((points, channels), lambda b, *_: (0, 0)),
                pl.BlockSpec((head_rows, width), lambda b, *_: (b, 0)),
                pl.BlockSpec((node_rows, width), lambda b, *_: (0, 0)),
            ],
            out_specs=pl.BlockSpec((1, BLOCK + head_rows, channels), lambda b, *_: (b, 0, 0)),
            scratch_shapes=[pltpu.VMEM((points, BLOCK), jnp.float32)],
        ),
        out_shape=jax.ShapeDtypeStruct((blocks, BLOCK + head_rows, channels), jnp.bfloat16),
        compiler_params=pltpu.CompilerParams(vmem_limit_bytes=VMEM_LIMIT),
        cost_estimate=pl.CostEstimate(
            flops=2 * blocks * slots * points * BLOCK, bytes_accessed=2 * points * channels, transcendentals=0
        ),
    )(
        count,
        base,
        source.reshape(blocks, 1, slots),
        target.reshape(blocks, 1, slots),
        local_grid,
        w_output,
        local_cot,
    )


def edges_kernel(count_ref, source_ref, target_ref, out_ref):
    block = pl.program_id(0)
    nodes = out_ref.shape[0]
    slots = source_ref.shape[2]
    slot = lax.broadcasted_iota(jnp.int32, (1, slots), 1)
    target = jnp.where(slot < count_ref[block], target_ref[0], -1)
    node_rows = lax.broadcasted_iota(jnp.int32, (BLOCK, slots), 0)
    to_node = jnp.where(node_rows == target, 1.0, 0.0).astype(jnp.bfloat16)
    from_rows = lax.broadcasted_iota(jnp.int32, (nodes, slots), 0)
    from_node = jnp.where(from_rows == source_ref[0], 1.0, 0.0).astype(jnp.bfloat16)
    out_ref[...] = dot_nt(from_node, to_node).astype(jnp.bfloat16)
    start = pl.multiple_of(block * BLOCK, BLOCK)
    diagonal = lax.broadcasted_iota(jnp.int32, (BLOCK, BLOCK), 0) == lax.broadcasted_iota(
        jnp.int32, (BLOCK, BLOCK), 1
    )
    own = out_ref[pl.ds(start, BLOCK), :].astype(jnp.float32)
    out_ref[pl.ds(start, BLOCK), :] = (own + jnp.where(diagonal, 1.0, 0.0)).astype(jnp.bfloat16)


def edge_counts(source, target, count, nodes):
    blocks, slots = source.shape
    return pl.pallas_call(
        edges_kernel,
        grid_spec=pltpu.PrefetchScalarGridSpec(
            num_scalar_prefetch=1,
            grid=(blocks,),
            in_specs=[
                pl.BlockSpec((1, 1, slots), lambda b, *_: (b, 0, 0)),
                pl.BlockSpec((1, 1, slots), lambda b, *_: (b, 0, 0)),
            ],
            out_specs=pl.BlockSpec((nodes, BLOCK), lambda b, *_: (0, b)),
        ),
        out_shape=jax.ShapeDtypeStruct((nodes, nodes), jnp.bfloat16),
        compiler_params=pltpu.CompilerParams(vmem_limit_bytes=VMEM_LIMIT),
        cost_estimate=pl.CostEstimate(
            flops=2 * nodes * blocks * slots * BLOCK * 2, bytes_accessed=2 * nodes * nodes, transcendentals=0
        ),
    )(count, source.reshape(blocks, 1, slots), target.reshape(blocks, 1, slots))


def attention_kernel(
    index_ref,
    encoded_ref,
    w_encoder_ref,
    w_head_ref,
    received_ref,
    pairs_ref,
    left_ref,
    grads_ref,
    hidden_s,
    query_s,
    key_s,
    value_s,
    grad_s,
    queryt_s,
    keyt_s,
    valuet_s,
    gradt_s,
    encodedt_s,
    expo_s,
    dattn_s,
    attn_s,
    dscore_s,
    grad_qt_s,
    grad_k_s,
    grad_v_s,
):
    step = pl.program_id(0)
    blocks, block_rows, channels = encoded_ref.shape
    nodes = blocks * block_rows
    width = w_encoder_ref.shape[1]
    factor = 1.0 / math.sqrt(HD)

    @pl.when(step == 0)
    def _():
        def one_rows(index, carry):
            rows = pl.ds(pl.multiple_of(index * ROW_CHUNK, ROW_CHUNK), ROW_CHUNK)
            pair = ROW_CHUNK // block_rows
            encoded = encoded_ref[pl.ds(index * pair, pair)].reshape(ROW_CHUNK, channels)
            hidden = dot_nn(encoded, w_encoder_ref[...]).astype(jnp.bfloat16)
            hidden_s[rows, :] = hidden
            mixed = dot_nn(hidden, w_head_ref[...])
            query_s[rows, :] = mixed[:, :HD].astype(jnp.bfloat16)
            key_s[rows, :] = mixed[:, HD : 2 * HD].astype(jnp.bfloat16)
            value_s[rows, :] = mixed[:, 2 * HD :].astype(jnp.bfloat16)
            flipped = mixed.T
            queryt_s[:, rows] = flipped[:HD, :].astype(jnp.bfloat16)
            keyt_s[:, rows] = flipped[HD : 2 * HD, :].astype(jnp.bfloat16)
            valuet_s[:, rows] = flipped[2 * HD :, :].astype(jnp.bfloat16)
            return carry

        lax.fori_loop(0, nodes // ROW_CHUNK, one_rows, 0)
        for block in range(blocks):
            rows = slice(block * block_rows, (block + 1) * block_rows)
            gradt = received_ref[block, block_rows:, :]
            gradt_s[:, rows] = gradt
            grad_s[rows, :] = gradt.astype(jnp.float32).T.astype(jnp.bfloat16)
            encodedt_s[:, rows] = encoded_ref[block].astype(jnp.float32).T
        grad_k_s[...] = jnp.zeros_like(grad_k_s)
        grad_v_s[...] = jnp.zeros_like(grad_v_s)

    dest = pl.ds(pl.multiple_of(step * DEST_TILE, DEST_TILE), DEST_TILE)
    queryt = queryt_s[:, dest] * jnp.bfloat16(factor)
    gradt = gradt_s[:, dest]
    total = jnp.zeros((1, DEST_TILE), jnp.float32)
    weighted = jnp.zeros((1, DEST_TILE), jnp.float32)
    for index in range(nodes // ROW_CHUNK):
        rows = slice(index * ROW_CHUNK, (index + 1) * ROW_CHUNK)
        score = dot_nn(key_s[rows, :], queryt)
        times = pairs_ref[rows, :].astype(jnp.float32)
        expo = jnp.where(times > 0.0, jnp.exp(score), 0.0) * times
        dattn = dot_nn(value_s[rows, :], gradt)
        expo_s[rows, :] = expo
        dattn_s[rows, :] = dattn
        total += jnp.sum(expo, axis=0, keepdims=True)
        weighted += jnp.sum(expo * dattn, axis=0, keepdims=True)
    inverse = 1.0 / total
    mean_grad = weighted * inverse
    for index in range(nodes // ROW_CHUNK):
        rows = slice(index * ROW_CHUNK, (index + 1) * ROW_CHUNK)
        attn = expo_s[rows, :] * inverse
        attn_s[rows, :] = attn.astype(jnp.bfloat16)
        dscore_s[rows, :] = (attn * (dattn_s[rows, :] - mean_grad) * factor).astype(jnp.bfloat16)
    left_ref[:HD, :] = dot_nn(valuet_s[...], attn_s[...]).astype(jnp.bfloat16)
    own = left_ref.shape[0] - HD
    left_ref[HD:, :] = encodedt_s[
        pl.ds(pl.multiple_of(index_ref[0] * own, own), own), dest
    ].astype(jnp.bfloat16)
    grad_qt_s[:, dest] = dot_nn(keyt_s[...], dscore_s[...]).astype(jnp.bfloat16)
    grad_k_s[...] += dot_nn(dscore_s[...], query_s[dest, :])
    grad_v_s[...] += dot_nn(attn_s[...], grad_s[dest, :])

    @pl.when(step == pl.num_programs(0) - 1)
    def _():
        gradst = jnp.concatenate(
            [grad_qt_s[...], grad_k_s[...].T.astype(jnp.bfloat16), grad_v_s[...].T.astype(jnp.bfloat16)],
            axis=0,
        )
        parts = grads_ref.shape[0]
        piece = width // parts
        weights = dot_nn(gradst, hidden_s[...]).T.astype(jnp.bfloat16)
        grads_ref[:, :piece, :] = weights.reshape(parts, piece, 3 * HD)
        terms = dot_nn(gradst, encoded_ref[...].reshape(nodes, channels)).T.astype(jnp.bfloat16)
        own_rows = channels // parts
        for part in range(parts):
            grads_ref[part, piece:, :] = terms[part * own_rows : (part + 1) * own_rows, :]


def attention(index, encoded, w_encoder, w_head, received, pairs, parts):
    blocks, block_rows, channels = encoded.shape
    nodes = blocks * block_rows
    width = w_encoder.shape[1]
    whole = lambda *shape: pl.BlockSpec(shape, lambda j, *_: (0,) * len(shape))
    half, full = jnp.bfloat16, jnp.float32
    rows = HD + channels // parts
    return pl.pallas_call(
        attention_kernel,
        grid_spec=pltpu.PrefetchScalarGridSpec(
            num_scalar_prefetch=1,
            grid=(nodes // DEST_TILE,),
            in_specs=[
                whole(blocks, block_rows, channels),
                whole(channels, width),
                whole(width, 3 * HD),
                whole(*received.shape),
                pl.BlockSpec((nodes, DEST_TILE), lambda j, *_: (0, j)),
            ],
            out_specs=[
                pl.BlockSpec((rows, DEST_TILE), lambda j, *_: (0, j)),
                whole(parts, rows, 3 * HD),
            ],
            scratch_shapes=[
                pltpu.VMEM((nodes, width), half),
                pltpu.VMEM((nodes, HD), half),
                pltpu.VMEM((nodes, HD), half),
                pltpu.VMEM((nodes, HD), half),
                pltpu.VMEM((nodes, HD), half),
                pltpu.VMEM((HD, nodes), half),
                pltpu.VMEM((HD, nodes), half),
                pltpu.VMEM((HD, nodes), half),
                pltpu.VMEM((HD, nodes), half),
                pltpu.VMEM((channels, nodes), full),
                pltpu.VMEM((nodes, DEST_TILE), full),
                pltpu.VMEM((nodes, DEST_TILE), full),
                pltpu.VMEM((nodes, DEST_TILE), half),
                pltpu.VMEM((nodes, DEST_TILE), half),
                pltpu.VMEM((HD, nodes), half),
                pltpu.VMEM((nodes, HD), full),
                pltpu.VMEM((nodes, HD), full),
            ],
        ),
        out_shape=[
            jax.ShapeDtypeStruct((rows, nodes), half),
            jax.ShapeDtypeStruct((parts, rows, 3 * HD), half),
        ],
        compiler_params=pltpu.CompilerParams(vmem_limit_bytes=VMEM_LIMIT),
        cost_estimate=pl.CostEstimate(
            flops=12 * nodes * nodes * HD, bytes_accessed=2 * nodes * nodes, transcendentals=nodes * nodes
        ),
    )(index, encoded, w_encoder, w_head, received, pairs)


def meet_kernel(left_ref, cot_ref, grads_ref, out_ref):
    met = dot_nn(left_ref[...], cot_ref[...]).astype(jnp.bfloat16)
    parts = grads_ref.shape[0]
    piece = met.shape[1] // parts
    for part in range(parts):
        out_ref[part] = jnp.concatenate(
            [grads_ref[part], met[:, part * piece : (part + 1) * piece]], axis=1
        )


def meet(left, all_cot, grads):
    rows, nodes = left.shape
    width = all_cot.shape[1]
    parts, _, columns = grads.shape
    tiles = 4
    piece = width // parts
    return pl.pallas_call(
        meet_kernel,
        grid=(tiles,),
        in_specs=[
            pl.BlockSpec((rows, nodes), lambda j: (0, 0)),
            pl.BlockSpec((nodes, width // tiles), lambda j: (0, j)),
            pl.BlockSpec((parts // tiles, rows, columns), lambda j: (j, 0, 0)),
        ],
        out_specs=pl.BlockSpec((parts // tiles, rows, columns + piece), lambda j: (j, 0, 0)),
        out_shape=jax.ShapeDtypeStruct((parts, rows, columns + piece), jnp.bfloat16),
        compiler_params=pltpu.CompilerParams(vmem_limit_bytes=VMEM_LIMIT),
        cost_estimate=pl.CostEstimate(
            flops=2 * rows * nodes * width, bytes_accessed=2 * nodes * width, transcendentals=0
        ),
    )(left, all_cot, grads)


def finish_kernel(
    norm, sums_ref, w_query_ref, w_key_ref, w_value_ref, query_ref, key_ref, value_ref, output_ref, encoder_ref
):
    parts, rows, _ = sums_ref.shape
    outs = (query_ref, key_ref, value_ref, output_ref)
    for part in range(parts):
        piece = sums_ref[part].astype(jnp.float32) * norm
        columns = slice(part * HD, (part + 1) * HD)
        for place, out in enumerate(outs):
            out[:, columns] = piece[:HD, place * HD : (place + 1) * HD]
        encoder_ref[:, columns] = piece[HD:, 3 * HD :]
    encoder = encoder_ref[...]
    for place, weight in enumerate((w_query_ref, w_key_ref, w_value_ref)):
        terms = jnp.concatenate(
            [sums_ref[part, HD:, place * HD : (place + 1) * HD] for part in range(parts)], axis=1
        )
        encoder += dot_nt(terms, weight[...]) * norm
    encoder_ref[...] = encoder


def finish(sums, w_query, w_key, w_value, norm):
    parts, rows, _ = sums.shape
    width = w_query.shape[0]
    full = jnp.float32
    return pl.pallas_call(
        functools.partial(finish_kernel, norm),
        out_shape=[jax.ShapeDtypeStruct((HD, width), full)] * 4
        + [jax.ShapeDtypeStruct((rows - HD, width), full)],
        compiler_params=pltpu.CompilerParams(vmem_limit_bytes=VMEM_LIMIT),
    )(sums, w_query, w_key, w_value)


def spread(array, axis):
    size = lax.axis_size(axis)
    copies = jnp.broadcast_to(array[None], (size,) + array.shape)
    return lax.all_to_all(copies, axis, split_axis=0, concat_axis=0, tiled=True)


def per_device(
    grid_fields,
    cotangent,
    encoder_source,
    encoder_target,
    encoder_count,
    mesh_source,
    mesh_target,
    mesh_count,
    w_encoder,
    w_query,
    w_key,
    w_value,
    w_output,
):
    model_size = lax.axis_size("mp")
    data_size = lax.axis_size("dp")
    model_index = lax.axis_index("mp")
    local_grid = grid_fields[0]
    local_cot = cotangent[0]
    points, channels = local_grid.shape
    node_rows, width = local_cot.shape
    nodes = node_rows * model_size
    half = jnp.bfloat16

    other = lax.ppermute(local_cot, "mp", [(i, i ^ 1) for i in range(model_size)])
    odd = model_index % 2 == 1
    both = jnp.concatenate([jnp.where(odd, other, local_cot), jnp.where(odd, local_cot, other)], axis=0)
    lanes = [list(range(first, model_size, 2)) for first in range(2)]
    all_cot = lax.all_gather(both, "mp", axis=0, tiled=True, axis_index_groups=lanes)

    partials = encoder_partials(
        local_grid,
        encoder_source,
        encoder_target,
        encoder_count,
        (model_index * points).reshape(1).astype(jnp.int32),
        w_output,
        local_cot,
    )
    received = lax.all_to_all(partials, "mp", split_axis=0, concat_axis=0, tiled=True)
    own_encoded = jnp.sum(received[:, :node_rows].astype(jnp.float32), axis=0).astype(half)
    encoded = spread(own_encoded, "mp")

    pairs = edge_counts(mesh_source, mesh_target, mesh_count, nodes)
    first = model_index * HD
    w_head = jnp.concatenate(
        [lax.dynamic_slice_in_dim(item, first, HD, 1) for item in (w_query, w_key, w_value)], axis=1
    )
    left, grads = attention(
        model_index.reshape(1).astype(jnp.int32), encoded, w_encoder, w_head, received, pairs, data_size
    )
    shares = meet(left, all_cot, grads)

    shares = lax.all_to_all(shares, "dp", split_axis=0, concat_axis=0, tiled=True)
    share = jnp.sum(shares.astype(jnp.float32), axis=0).astype(half)
    across = [
        (data * model_size + model, model * model_size + data)
        for data in range(data_size)
        for model in range(model_size)
    ]
    swapped = lax.ppermute(share, ("dp", "mp"), across)
    column = lax.broadcasted_iota(jnp.int32, share.shape, 1)
    share = jnp.where(column < 3 * HD, swapped, share)
    sums = spread(share, "dp")
    norm = 1.0 / math.sqrt(data_size * nodes)
    return tuple(finish(sums, w_query, w_key, w_value, norm))


def solution(mesh):
    in_specs = (
        P("dp", "mp", None),
        P("dp", "mp", None),
        P(),
        P(),
        P(),
        P(),
        P(),
        P(),
        P(),
        P(),
        P(),
        P(),
        P(),
    )
    out_specs = (P("mp", None), P("mp", None), P("mp", None), P("mp", None), P("mp", None))
    return jax.shard_map(
        per_device, mesh=mesh, in_specs=in_specs, out_specs=out_specs, check_vma=False
    )
```

time: 1480 us -> 205 us (0.14)
  waiting for transfers between devices: 610 us -> 35.7 us
  other arithmetic: 406 us -> 4.17 us
  local copies, waits for them, and re-layouts: 275 us -> 13.6 us
  blocking collectives: 125 us -> 46.6 us
  Pallas kernels: 0 us -> 70 us
  matrix products: 24.8 us -> 0 us
    reduce_scatter x5 -> x0, waiting for transfers between devices: 414 us -> none  [spread_sum(): lax.psum_scatter(column_terms(left, right), 'mp', scatter_dimension=0, ti...]
    scatter-add x24 -> x0, other arithmetic: 354 us -> none  [the longest x4 62.1 us: one_group(): grad_v_sum = grad_v_sum.at[sources].add(value_terms)]
    gather x25 -> x0, local copies, waits for them, and re-layouts: 242 us -> none  [the longest x4 52.8 us: one_group(): mean_grad[local_dest]]
    all_gather x1, waiting for transfers between devices: 88.4 us -> 0.01 us  [per_device(): lax.all_gather(both, 'mp', axis=0, tiled=True, axis_index_groups=lanes)]
    psum x1 -> x0, waiting for transfers between devices: 86.4 us -> none  [per_device(): lax.psum((part_query, part_key, part_value, part_output, part_encoder), '...]
    psum x1 -> x0, blocking collectives: 71.8 us -> none  [per_device(): lax.psum((part_query, part_key, part_value, part_output, part_encoder), '...]
    pallas_call x0 -> x5, Pallas kernels: none -> 70 us  [the longest x1 25.5 us: attention(): pl.pallas_call(attention_kernel, grid_spec=pltpu.PrefetchScalarGridSpec(n...]
    dot_general x13 -> x0, matrix products: 24.8 us -> none  [the longest x5 15 us: column_terms(): lax.dot_general(left, right, (((0,), (0,)), ((), ())), preferred_element_...]
  transfers between devices with their start and end apart: 11 -> 5, of which waited for: 10 -> 4; matrix products, arithmetic and copies ran while one was open for 3% -> 3% of each run, Pallas kernels for 0% -> 31%
where the time goes in v1:
time: 205 us; the launch traced here: 204 us
  Pallas kernels  70 us (34%)
  blocking collectives  46.6 us (23%)
  waiting for transfers between devices  35.7 us (17%)
  starting transfers between devices  19.7 us (10%)
  between operations  14.3 us (7%)
  local copies, waits for them, and re-layouts  13.6 us (7%)
  other arithmetic  4.17 us (2%)
    all_to_all x1, waiting for transfers between devices, per_device(): lax.all_to_all(partials, 'mp', split_axis=0, concat_axis=0, tiled=True)  27.3 us
    pallas_call x1, Pallas kernels, attention(): pl.pallas_call(attention_kernel, grid_spec=pltpu.PrefetchScalarGridSpec(n...  25.5 us
    all_to_all x1, blocking collectives, spread(): return lax.all_to_all(copies, axis, split_axis=0, concat_axis=0, tiled=True)  24.2 us
    pallas_call x1, Pallas kernels, encoder_partials(): pl.pallas_call(encoder_kernel, grid_spec=pltpu.PrefetchScalarGridSpec(num...  24.1 us
    all_to_all x1, blocking collectives, per_device(): lax.all_to_all(shares, 'dp', split_axis=0, concat_axis=0, tiled=True)  22.4 us
    pallas_call x1, Pallas kernels, edge_counts(): pl.pallas_call(edges_kernel, grid_spec=pltpu.PrefetchScalarGridSpec(num_s...  14.1 us
    all_to_all x1, starting transfers between devices, per_device(): lax.all_to_all(partials, 'mp', split_axis=0, concat_axis=0, tiled=True)  10.4 us
    unnamed x38, local copies, waits for them, and re-layouts  10.2 us
  transfers between devices with their start and end apart: 5, of which 4 were waited for; matrix products, arithmetic and copies ran while one was open for 3% of the time, Pallas kernels for 31%

profile of v1, /device:TPU:1, one launch (start us, length us, event | category | flops | bytes accessed | tf_op | source)
XLA Modules:
  0.0 204.0 jit_solution(6515629210694850350)
XLA Ops:
  7.2 0.0 copy-start.9
  7.2 0.0 copy-start.15
  7.2 0.0 copy-start.16
  7.2 0.0 copy-start.11
  7.2 0.0 copy-start.13
  7.2 0.0 copy-start.10
  7.2 0.0 all-gather.2.cloned.1.call-start
  7.3 2.2 %collective-permute-start = (bf16[128,1024]{1,0:T(8,128)(2,1)}, bf16[128,1024]{1,0:T(8,128)(2,1)S(1)}, u32[]{:S(2)}, u32[]{:S(2)}) collective-permute-start(bf16[128,1024]{1,0:T(8,128)(2,1)} %bitcast.6), channel_id=1, source_target_pairs={{0,1},{1,0},{2,3},{3,2},{4,5},{5,4},{6,7},{7,6},{8,9},{9,8},{10,11... | collective-permute-start | bytes 786440 | tf_op jit(solution)/shard_map/ppermute | solution.py:395
  9.5 5.1 %collective-permute-done = bf16[128,1024]{1,0:T(8,128)(2,1)S(1)} collective-permute-done((bf16[128,1024]{1,0:T(8,128)(2,1)}, bf16[128,1024]{1,0:T(8,128)(2,1)S(1)}, u32[]{:S(2)}, u32[]{:S(2)}) %collective-permute-start) | collective-permute-done | bytes 262176 | tf_op jit(solution)/shard_map/ppermute | solution.py:395
  14.6 1.0 broadcast_select_fusion.1
  15.6 0.9 pad_maximum_fusion.1
  16.5 0.0 all-gather.2.cloned.1.call-update
  16.5 0.0 copy-done.15
  16.5 0.1 reshape.32.source_ref
  16.6 0.0 copy-done.16
  16.6 0.1 reshape.33.target_ref
  16.7 0.0 copy-done.9
  16.8 0.0 copy-done.11
  16.8 0.0 copy-done.13
  16.8 0.0 copy-done.10
  16.8 24.1 %shard_map.164 = bf16[16,192,128]{2,1,0:T(8,128)(2,1)S(1)} custom-call(s32[16]{0:T(128)S(1)} %copy-done.13, s32[1]{0:T(128)} %bitcast.1.base_ref, s32[16,1,2048]{2,1,0:T(1,128)S(1)} %reshape.32.source_ref, s32[16,1,2048]{2,1,0:T(1,128)S(1)} %reshape.33.target_ref, bf16[1024,128]{1,0:T(8,128)(2,1)S(1)} %bitcast.8, bf16[1024,1024]{1,0:T(8,128)(2,1)S(1)} %copy-done.10, ...), custom_call_target="tpu_custom_call" | custom-call | flops 8589934592 | bytes 262144 | tf_op jit(solution)/shard_map/pallas_call | solution.py:66
  40.9 0.0 copy-start.3
  40.9 0.9 copy-done.3
  41.8 0.0 copy-start.1
  41.8 10.4 %all-to-all-start = ((bf16[16,192,128]{2,1,0:T(8,128)(2,1)}), bf16[16,192,128]{2,1,0:T(8,128)(2,1)S(1)}, u32[]{:S(2)}, u32[]{:S(2)}) async-start(bf16[16,192,128]{2,1,0:T(8,128)(2,1)} %copy-done.3), calls=%async_computation | async-start | bytes 1572864 | tf_op jit(solution)/shard_map/all_to_all | solution.py:410
  52.2 0.0 copy-start.17
  52.2 0.0 copy-start.18
  52.2 2.1 %constant_dynamic-slice_fusion = (bf16[1024,64]{1,0:T(8,128)(2,1)}, bf16[1024,64]{1,0:T(8,128)(2,1)}) fusion(bf16[1024,1024]{1,0:T(8,128)(2,1)} %w_value_ref.1, s32[]{:T(128)S(6)} %select_n.28, bf16[1024,1024]{1,0:T(8,128)(2,1)} %w_key_ref.1), kind=kLoop, calls=%fused_computation.7 | loop fusion | bytes 524292 | tf_op jit(solution)/shard_map/dynamic_slice | solution.py:417
  54.3 0.0 copy-start.14
  54.3 27.3 %all-to-all-done.received_ref = bf16[16,192,128]{2,1,0:T(8,128)(2,1)S(1)} async-done(((bf16[16,192,128]{2,1,0:T(8,128)(2,1)}), bf16[16,192,128]{2,1,0:T(8,128)(2,1)S(1)}, u32[]{:S(2)}, u32[]{:S(2)}) %all-to-all-start) | async-done | bytes 786464 | tf_op jit(solution)/shard_map/all_to_all | solution.py:410
  81.6 0.1 slice_reduce_fusion
  81.6 0.9 broadcast_in_dim.4
  82.5 4.8 %all-to-all-start.1 = ((bf16[16,128,128]{2,1,0:T(8,128)(2,1)}), bf16[16,128,128]{2,1,0:T(8,128)(2,1)S(1)}, u32[]{:S(2)}, u32[]{:S(2)}) async-start(bf16[16,128,128]{2,1,0:T(8,128)(2,1)} %broadcast_in_dim.4), calls=%async_computation.1 | async-start | bytes 1048576 | tf_op jit(solution)/shard_map/all_to_all | solution.py:367
  87.3 0.0 copy-done.1
  87.3 0.2 constant_dynamic-slice_fusion.2
  87.5 0.0 copy-done.17
  87.5 0.0 copy-done.18
  87.6 2.1 %pad_maximum_fusion.w_head_ref = bf16[1024,192]{1,0:T(8,128)(2,1)} fusion(bf16[1024,64]{1,0:T(8,128)(2,1)} %get-tuple-element.11, bf16[1024,64]{1,0:T(8,128)(2,1)} %get-tuple-element.12, bf16[1024,64]{1,0:T(8,128)(2,1)S(1)} %constant_dynamic-slice_fusion.2), kind=kLoop, calls=%fused_computation.1 | loop fusion | flops 1179648 | bytes 786432 | tf_op jit(solution)/shard_map/concatenate | solution.py:416
  89.7 0.0 copy-done.14
  89.7 14.1 %shard_map.165.pairs_ref = bf16[2048,2048]{1,0:T(8,128)(2,1)} custom-call(s32[16]{0:T(128)S(1)} %copy-done.14, s32[16,1,512]{2,1,0:T(1,128)S(1)} %reshape.34.source_ref, s32[16,1,512]{2,1,0:T(1,128)S(1)} %reshape.35.target_ref), custom_call_target="tpu_custom_call" | custom-call | flops 8589934592 | bytes 8388608 | tf_op jit(solution)/shard_map/pallas_call | solution.py:118
  103.8 0.3 all-to-all-done.1.encoded_ref
  104.0 0.0 copy-start.4
  104.0 0.8 copy-done.4
  104.8 1.0 copy-done.5
  105.9 0.0 copy-start.6
  105.9 1.0 copy-done.6
  106.9 0.0 copy-start.12
  106.9 0.9 copy-done.12
  107.8 25.5 %shard_map.166 = (bf16[72,2048]{1,0:T(8,128)(2,1)S(1)}, bf16[16,72,192]{2,1,0:T(8,128)(2,1)S(1)}) custom-call(s32[1]{0:T(128)} %bitcast.index_ref, bf16[16,128,128]{2,1,0:T(8,128)(2,1)S(1)} %copy-done.5, bf16[128,1024]{1,0:T(8,128)(2,1)S(1)} %copy-done.12, bf16[1024,192]{1,0:T(8,128)(2,1)S(1)} %copy-done.6, ...), custom_call_target="tpu_custom_call" | custom-call | flops 3221225472 | bytes 8388608 | tf_op jit(solution)/shard_map/pallas_call | solution.py:252
  133.4 0.0 copy-start.7
  133.4 0.7 copy-done.7
  134.1 0.0 all-gather.2.cloned.1.call-done.cot_ref
  134.1 0.0 copy-start
  134.1 2.2 %copy-done = bf16[2048,1024]{1,0:T(8,128)(2,1)S(1)} copy-done((bf16[2048,1024]{1,0:T(8,128)(2,1)S(1)}, bf16[2048,1024]{1,0:T(8,128)(2,1)}, u32[]{:S(2)}) %copy-start) | copy-done | bytes 4194328
  136.3 0.0 copy-start.8
  136.3 1.0 copy-done.8
  137.3 2.1 %shard_map.167 = bf16[16,72,256]{2,1,0:T(8,128)(2,1)S(1)} custom-call(bf16[72,2048]{1,0:T(8,128)(2,1)S(1)} %copy-done.8, bf16[2048,1024]{1,0:T(8,128)(2,1)S(1)} %copy-done, bf16[16,72,192]{2,1,0:T(8,128)(2,1)S(1)} %get-tuple-element.8.grads_ref), custom_call_target="tpu_custom_call" | custom-call | flops 301989888 | bytes 4194304 | tf_op jit(solution)/shard_map/pallas_call | solution.py:315
  139.4 22.4 %all_to_all.20 = bf16[16,72,256]{2,1,0:T(8,128)(2,1)S(1)} all-to-all(bf16[16,72,256]{2,1,0:T(8,128)(2,1)S(1)} %shard_map.167), channel_id=1, replica_groups=mesh['dp'=16,'mp'=16] {'dp'}, dimensions={0} | all-to-all | bytes 1179648 | tf_op jit(solution)/shard_map/all_to_all | solution.py:424
  161.8 0.1 reduce_sum.25
  161.9 2.2 %collective-permute-start.1 = (bf16[72,256]{1,0:T(8,128)(2,1)S(1)}, bf16[72,256]{1,0:T(8,128)(2,1)S(1)}, u32[]{:S(2)}, u32[]{:S(2)}) collective-permute-start(bf16[72,256]{1,0:T(8,128)(2,1)S(1)} %reduce_sum.25), channel_id=1, source_target_pairs={{0,0},{1,16},{2,32},{3,48},{4,64},{5,80},{6,96},{7,112},{8,128},{9... | collective-permute-start | bytes 110600 | tf_op jit(solution)/shard_map/ppermute | solution.py:431
  164.1 3.0 %collective-permute-done.1 = bf16[72,256]{1,0:T(8,128)(2,1)S(1)} collective-permute-done((bf16[72,256]{1,0:T(8,128)(2,1)S(1)}, bf16[72,256]{1,0:T(8,128)(2,1)S(1)}, u32[]{:S(2)}, u32[]{:S(2)}) %collective-permute-start.1) | collective-permute-done | bytes 36896 | tf_op jit(solution)/shard_map/ppermute | solution.py:431
  167.2 24.2 %all_to_all.21.sums_ref = bf16[16,72,256]{2,1,0:T(8,128)(2,1)S(1)} all-to-all(bf16[16,72,256]{2,1,0:T(8,128)(2,1)S(1)} %broadcast_in_dim.5), channel_id=1, replica_groups=mesh['dp'=16,'mp'=16] {'dp'}, dimensions={0} | all-to-all | bytes 1179648 | tf_op jit(solution)/shard_map/all_to_all | solution.py:367
  191.4 1.6 copy-done.2
  193.0 4.2 %shard_map.168 = (f32[64,1024]{1,0:T(8,128)}, f32[64,1024]{1,0:T(8,128)}, f32[64,1024]{1,0:T(8,128)}, f32[64,1024]{1,0:T(8,128)}, f32[8,1024]{1,0:T(8,128)}) custom-call(bf16[16,72,256]{2,1,0:T(8,128)(2,1)S(1)} %all_to_all.21.sums_ref, bf16[1024,1024]{1,0:T(8,128)(2,1)S(1)} %copy-done.1, bf16[1024,1024]{1,0:T(8,128)(2,1)S(1)} %copy-done.2, ...), custom_call_target="tpu_custom_call" | custom-call | tf_op jit(solution)/shard_map/pallas_call | solution.py:356
  (7 shorter events, 0.1 us)
Async XLA Ops:
  7.2 9.6 %copy-start.9 = (bf16[1,128,1024]{2,1,0:T(8,128)(2,1)S(1)}, bf16[1,128,1024]{2,1,0:T(8,128)(2,1)}, u32[]{:S(2)}) copy-start(bf16[1,128,1024]{2,1,0:T(8,128)(2,1)} %param.14) | copy-start | bytes 786436
  7.2 9.4 %copy-start.15 = (s32[16,2048]{1,0:T(8,128)S(1)}, s32[16,2048]{1,0:T(8,128)}, u32[]{:S(2)}) copy-start(s32[16,2048]{1,0:T(8,128)} %param.15) | copy-start | bytes 393220
  7.2 9.4 %copy-start.16 = (s32[16,2048]{1,0:T(8,128)S(1)}, s32[16,2048]{1,0:T(8,128)}, u32[]{:S(2)}) copy-start(s32[16,2048]{1,0:T(8,128)} %param.16) | copy-start | bytes 393220
  7.2 9.6 %copy-start.11 = (bf16[1,1024,128]{2,1,0:T(8,128)(2,1)S(1)}, bf16[1,1024,128]{2,1,0:T(8,128)(2,1)}, u32[]{:S(2)}) copy-start(bf16[1,1024,128]{2,1,0:T(8,128)(2,1)} %param.13) | copy-start | bytes 786436
  7.2 9.6 %copy-start.13 = (s32[16]{0:T(128)S(1)}, s32[16]{0:T(128)}, u32[]{:S(2)}) copy-start(s32[16]{0:T(128)} %count_ref.2) | copy-start | bytes 196
  7.2 9.6 %copy-start.10 = (bf16[1024,1024]{1,0:T(8,128)(2,1)S(1)}, bf16[1024,1024]{1,0:T(8,128)(2,1)}, u32[]{:S(2)}) copy-start(bf16[1024,1024]{1,0:T(8,128)(2,1)} %w_output_ref.1) | copy-start | bytes 6291460
  7.2 126.9 %all-gather.2.cloned.1.call-start = ((), (), s32[]{:S(2)}) async-start(), calls=%async_computation.4 | async-start | bytes 4718592 | tf_op jit(solution)/shard_map/all_gather | solution.py:399
  7.3 7.3 %collective-permute-start = (bf16[128,1024]{1,0:T(8,128)(2,1)}, bf16[128,1024]{1,0:T(8,128)(2,1)S(1)}, u32[]{:S(2)}, u32[]{:S(2)}) collective-permute-start(bf16[128,1024]{1,0:T(8,128)(2,1)} %bitcast.6), channel_id=1, source_target_pairs={{0,1},{1,0},{2,3},{3,2},{4,5},{5,4},{6,7},{7,6},{8,9},{9,8},{10,11... | collective-permute-start | bytes 786440 | tf_op jit(solution)/shard_map/ppermute | solution.py:395
  40.9 0.9 copy-start.3
  41.8 45.6 %copy-start.1 = (bf16[1024,1024]{1,0:T(8,128)(2,1)S(1)}, bf16[1024,1024]{1,0:T(8,128)(2,1)}, u32[]{:S(2)}) copy-start(bf16[1024,1024]{1,0:T(8,128)(2,1)} %w_query_ref.1) | copy-start | bytes 6291460
  41.8 39.8 %all-to-all-start = ((bf16[16,192,128]{2,1,0:T(8,128)(2,1)}), bf16[16,192,128]{2,1,0:T(8,128)(2,1)S(1)}, u32[]{:S(2)}, u32[]{:S(2)}) async-start(bf16[16,192,128]{2,1,0:T(8,128)(2,1)} %copy-done.3), calls=%async_computation | async-start | bytes 1572864 | tf_op jit(solution)/shard_map/all_to_all | solution.py:410
  52.2 35.3 %copy-start.17 = (s32[16,512]{1,0:T(8,128)S(1)}, s32[16,512]{1,0:T(8,128)}, u32[]{:S(2)}) copy-start(s32[16,512]{1,0:T(8,128)} %param.18) | copy-start | bytes 98308
  52.2 35.3 %copy-start.18 = (s32[16,512]{1,0:T(8,128)S(1)}, s32[16,512]{1,0:T(8,128)}, u32[]{:S(2)}) copy-start(s32[16,512]{1,0:T(8,128)} %param.19) | copy-start | bytes 98308
  54.3 35.4 %copy-start.14 = (s32[16]{0:T(128)S(1)}, s32[16]{0:T(128)}, u32[]{:S(2)}) copy-start(s32[16]{0:T(128)} %count_ref.3) | copy-start | bytes 196
  82.5 21.5 %all-to-all-start.1 = ((bf16[16,128,128]{2,1,0:T(8,128)(2,1)}), bf16[16,128,128]{2,1,0:T(8,128)(2,1)S(1)}, u32[]{:S(2)}, u32[]{:S(2)}) async-start(bf16[16,128,128]{2,1,0:T(8,128)(2,1)} %broadcast_in_dim.4), calls=%async_computation.1 | async-start | bytes 1048576 | tf_op jit(solution)/shard_map/all_to_all | solution.py:367
  104.0 0.8 copy-start.4
  104.8 1.0 copy-start.5
  105.9 1.0 copy-start.6
  106.9 0.9 copy-start.12
  133.4 0.7 copy-start.7
  134.1 2.2 %copy-start = (bf16[2048,1024]{1,0:T(8,128)(2,1)S(1)}, bf16[2048,1024]{1,0:T(8,128)(2,1)}, u32[]{:S(2)}) copy-start(bf16[2048,1024]{1,0:T(8,128)(2,1)} %all-gather.2.cloned.1.call-done.cot_ref) | copy-start | bytes 12582916
  136.3 1.0 copy-start.8
  161.9 5.3 %collective-permute-start.1 = (bf16[72,256]{1,0:T(8,128)(2,1)S(1)}, bf16[72,256]{1,0:T(8,128)(2,1)S(1)}, u32[]{:S(2)}, u32[]{:S(2)}) collective-permute-start(bf16[72,256]{1,0:T(8,128)(2,1)S(1)} %reduce_sum.25), channel_id=1, source_target_pairs={{0,0},{1,16},{2,32},{3,48},{4,64},{5,80},{6,96},{7,112},{8,128},{9... | collective-permute-start | bytes 110600 | tf_op jit(solution)/shard_map/ppermute | solution.py:431
  191.4 1.6 copy-start.2
Sparse Core Ops, SparseCore 0:
  16.6 77.5 all-gather.1

commit v2 on v1

v2 whole, which is shorter than its diff:
```python
import functools
import math

import jax
import jax.numpy as jnp
from jax import lax
from jax.experimental import pallas as pl
from jax.experimental.pallas import tpu as pltpu
from jax.sharding import PartitionSpec as P

BLOCK = 128
HD = 64
LOW = 256
FIRST_SLOTS = 1024
EDGE_BLOCKS = 4
DEST_TILE = 256
ROW_CHUNK = 256
MEET_TILES = 4
WIDE = 60 * 1024 * 1024
SMALL = 12 * 1024 * 1024
ROOM = 24 * 1024 * 1024
half = jnp.bfloat16
full = jnp.float32


def dot_nn(left, right):
    return lax.dot_general(left, right, (((1,), (0,)), ((), ())), preferred_element_type=full)


def dot_nt(left, right):
    return lax.dot_general(left, right, (((1,), (1,)), ((), ())), preferred_element_type=full)


def whole(*shape):
    return pl.BlockSpec(shape, lambda *_: (0,) * len(shape))


def one_hot(rows, index):
    place = lax.broadcasted_iota(jnp.int32, (rows, index.shape[1]), 0)
    return jnp.where(place == index, 1.0, 0.0).astype(half)


def encoder_kernel(
    count_ref, base_ref, source_ref, target_ref, grid_ref, w_output_ref, cot_ref, out_ref, pairs_ref, w_s, sem
):
    blocks = source_ref.shape[0]
    points = grid_ref.shape[0]
    highs = points // LOW
    base = base_ref[0]
    fetch = pltpu.make_async_copy(w_output_ref, w_s, sem)
    fetch.start()

    def pair_counts(block, first):
        source = source_ref[block : block + 1, pl.ds(first, FIRST_SLOTS)] - base
        target = target_ref[block : block + 1, pl.ds(first, FIRST_SLOTS)]
        slot = first + lax.broadcasted_iota(jnp.int32, (1, FIRST_SLOTS), 1)
        used = (slot < count_ref[block]) & (source >= 0) & (source < points)
        column = jnp.where(used, lax.shift_right_logical(source, 8) * BLOCK + target, -1)
        return dot_nt(one_hot(highs * BLOCK, column), one_hot(LOW, source & (LOW - 1)))

    for block in range(blocks):
        pairs_ref[block] = pair_counts(block, 0)
    for block in range(blocks):

        def more(step, carry, block=block):
            pairs_ref[block] += pair_counts(block, pl.multiple_of(step * FIRST_SLOTS, FIRST_SLOTS))
            return carry

        lax.fori_loop(1, (count_ref[block] + FIRST_SLOTS - 1) // FIRST_SLOTS, more, 0)
    for block in range(blocks):
        counts = pairs_ref[block].astype(half)
        sums = dot_nn(counts[:BLOCK], grid_ref[:LOW])
        for high in range(1, highs):
            sums += dot_nn(
                counts[high * BLOCK : (high + 1) * BLOCK], grid_ref[high * LOW : (high + 1) * LOW]
            )
        out_ref[block, :BLOCK, :] = sums.astype(half)
    fetch.wait()
    mixed = dot_nt(w_s[...], cot_ref[...]).astype(half)
    heads = mixed.shape[0] // blocks
    for block in range(blocks):
        out_ref[block, BLOCK:, :] = mixed[block * heads : (block + 1) * heads]


def encoder_partials(local_grid, source, target, count, base, w_output, local_cot):
    blocks, slots = source.shape
    points, channels = local_grid.shape
    node_rows, width = local_cot.shape
    head_rows = width // blocks
    return pl.pallas_call(
        encoder_kernel,
        grid_spec=pltpu.PrefetchScalarGridSpec(
            num_scalar_prefetch=2,
            grid=(1,),
            in_specs=[
                whole(blocks, slots),
                whole(blocks, slots),
                whole(points, channels),
                pl.BlockSpec(memory_space=pl.ANY),
                whole(node_rows, width),
            ],
            out_specs=whole(blocks, BLOCK + head_rows, channels),
            scratch_shapes=[
                pltpu.VMEM((blocks, points // LOW * BLOCK, LOW), full),
                pltpu.VMEM((width, width), half),
                pltpu.SemaphoreType.DMA,
            ],
        ),
        out_shape=jax.ShapeDtypeStruct((blocks, BLOCK + head_rows, channels), half),
        compiler_params=pltpu.CompilerParams(vmem_limit_bytes=WIDE),
        cost_estimate=pl.CostEstimate(
            flops=2 * blocks * slots * points * BLOCK, bytes_accessed=2 * points * channels, transcendentals=0
        ),
    )(count, base, source, target, local_grid, w_output, local_cot)


def collect_kernel(odd_ref, received_ref, own_ref, other_ref, copies_ref, both_ref):
    parts, rows, _ = copies_ref.shape
    total = received_ref[0, :rows, :].astype(full)
    for part in range(1, parts):
        total += received_ref[part, :rows, :].astype(full)
    total = total.astype(half)
    for part in range(parts):
        copies_ref[part] = total
    own, other = own_ref[...], other_ref[...]
    odd = odd_ref[0] == 1

    @pl.when(odd)
    def _():
        both_ref[:rows, :] = other
        both_ref[rows:, :] = own

    @pl.when(jnp.logical_not(odd))
    def _():
        both_ref[:rows, :] = own
        both_ref[rows:, :] = other


def collect(odd, received, own, other):
    parts, _, channels = received.shape
    rows, width = own.shape
    return pl.pallas_call(
        collect_kernel,
        grid_spec=pltpu.PrefetchScalarGridSpec(
            num_scalar_prefetch=1,
            grid=(1,),
            in_specs=[whole(*received.shape), whole(rows, width), whole(rows, width)],
            out_specs=[whole(parts, rows, channels), whole(2 * rows, width)],
        ),
        out_shape=[
            jax.ShapeDtypeStruct((parts, rows, channels), half),
            jax.ShapeDtypeStruct((2 * rows, width), half),
        ],
        compiler_params=pltpu.CompilerParams(vmem_limit_bytes=SMALL),
    )(odd, received, own, other)


def edges_kernel(count_ref, source_ref, target_ref, out_ref):
    slots = source_ref.shape[1]
    nodes, columns_here = out_ref.shape
    blocks = columns_here // BLOCK
    highs = nodes // LOW
    first_block = pl.program_id(0) * blocks
    slot = lax.broadcasted_iota(jnp.int32, (1, slots), 1)
    rows = lax.broadcasted_iota(jnp.int32, (LOW, BLOCK), 0)
    columns = lax.broadcasted_iota(jnp.int32, (LOW, BLOCK), 1)
    for block in range(blocks):
        source = source_ref[pl.ds(first_block + block, 1), :]
        target = target_ref[pl.ds(first_block + block, 1), :]
        used = slot < count_ref[first_block + block]
        column = jnp.where(used, lax.shift_right_logical(source, 8) * BLOCK + target, -1)
        counts = dot_nt(one_hot(LOW, source & (LOW - 1)), one_hot(highs * BLOCK, column))
        for high in range(highs):
            own = jnp.where(high * LOW + rows == (first_block + block) * BLOCK + columns, 1.0, 0.0)
            out_ref[high * LOW : (high + 1) * LOW, block * BLOCK : (block + 1) * BLOCK] = (
                counts[:, high * BLOCK : (high + 1) * BLOCK] + own
            ).astype(half)


def edge_counts(source, target, count, nodes):
    blocks, slots = source.shape
    some = EDGE_BLOCKS
    return pl.pallas_call(
        edges_kernel,
        grid_spec=pltpu.PrefetchScalarGridSpec(
            num_scalar_prefetch=1,
            grid=(blocks // some,),
            in_specs=[
                whole(blocks, slots),
                whole(blocks, slots),
            ],
            out_specs=pl.BlockSpec((nodes, some * BLOCK), lambda b, *_: (0, b)),
        ),
        out_shape=jax.ShapeDtypeStruct((nodes, nodes), half),
        compiler_params=pltpu.CompilerParams(vmem_limit_bytes=WIDE),
        cost_estimate=pl.CostEstimate(
            flops=2 * nodes * blocks * slots * BLOCK * 2, bytes_accessed=2 * nodes * nodes, transcendentals=0
        ),
    )(count, source, target)


def attention_kernel(
    index_ref,
    encoded_ref,
    w_encoder_ref,
    w_query_ref,
    w_key_ref,
    w_value_ref,
    received_ref,
    pairs_ref,
    left_ref,
    grads_ref,
    hidden_s,
    query_s,
    key_s,
    value_s,
    queryt_s,
    keyt_s,
    valuet_s,
    gradt_s,
    expo_s,
    dattn_s,
    grad_qt_s,
    grad_kv_s,
):
    step = pl.program_id(0)
    blocks, block_rows, channels = encoded_ref.shape
    nodes = blocks * block_rows
    width = w_encoder_ref.shape[1]
    factor = 1.0 / math.sqrt(HD)

    @pl.when(step == 0)
    def _():
        encoded = encoded_ref[...].reshape(nodes, channels)
        odd = index_ref[0] % 2 == 1
        w_head = jnp.concatenate(
            [jnp.where(odd, ref[:, HD:], ref[:, :HD]) for ref in (w_query_ref, w_key_ref, w_value_ref)], axis=1
        )
        for index in range(nodes // ROW_CHUNK):
            rows = slice(index * ROW_CHUNK, (index + 1) * ROW_CHUNK)
            hidden = dot_nn(encoded[rows], w_encoder_ref[...]).astype(half)
            hidden_s[rows, :] = hidden
            mixed = dot_nn(hidden, w_head)
            query_s[rows, :] = mixed[:, :HD].astype(half)
            key_s[rows, :] = mixed[:, HD : 2 * HD].astype(half)
            value_s[rows, :] = mixed[:, 2 * HD :].astype(half)
            flipped = mixed.T
            queryt_s[:, rows] = (flipped[:HD, :] * factor).astype(half)
            keyt_s[:, rows] = (flipped[HD : 2 * HD, :] * factor).astype(half)
            valuet_s[:, rows] = flipped[2 * HD :, :].astype(half)
        for block in range(blocks):
            gradt_s[:, block * block_rows : (block + 1) * block_rows] = received_ref[block, block_rows:, :]
        grad_kv_s[...] = jnp.zeros_like(grad_kv_s)

    dest = pl.ds(pl.multiple_of(step * DEST_TILE, DEST_TILE), DEST_TILE)
    queryt, gradt = queryt_s[:, dest], gradt_s[:, dest]
    query, grad = query_s[dest, :], gradt.astype(full).T.astype(half)
    none = jnp.zeros((DEST_TILE, HD), half)
    sides = jnp.concatenate([jnp.concatenate([query, none], axis=1), jnp.concatenate([none, grad], axis=1)], axis=0)
    total = jnp.zeros((1, DEST_TILE), full)
    weighted = jnp.zeros((1, DEST_TILE), full)
    for index in range(nodes // ROW_CHUNK):
        rows = slice(index * ROW_CHUNK, (index + 1) * ROW_CHUNK)
        score = dot_nn(key_s[rows, :], queryt)
        times = pairs_ref[rows, :].astype(full)
        expo = jnp.where(times > 0.0, jnp.exp(score), 0.0) * times
        dattn = dot_nn(value_s[rows, :], gradt)
        expo_s[rows, :] = expo
        dattn_s[rows, :] = dattn
        total += jnp.sum(expo, axis=0, keepdims=True)
        weighted += jnp.sum(expo * dattn, axis=0, keepdims=True)
    inverse = 1.0 / total
    mean_grad = weighted * inverse
    attended = jnp.zeros((HD, DEST_TILE), full)
    grad_qt = jnp.zeros((HD, DEST_TILE), full)
    for index in range(nodes // ROW_CHUNK):
        rows = slice(index * ROW_CHUNK, (index + 1) * ROW_CHUNK)
        attn = expo_s[rows, :] * inverse
        attn_round = attn.astype(half)
        dscore = (attn * (dattn_s[rows, :] - mean_grad)).astype(half)
        attended += dot_nn(valuet_s[:, rows], attn_round)
        grad_qt += dot_nn(keyt_s[:, rows], dscore)
        grad_kv_s[rows, :] += dot_nn(jnp.concatenate([dscore, attn_round], axis=1), sides)
    own = channels // grads_ref.shape[0]
    spare = left_ref.shape[0] - HD
    channel = lax.broadcasted_iota(jnp.int32, (spare, channels), 1)
    row = lax.broadcasted_iota(jnp.int32, (spare, channels), 0)
    pick = (channel == index_ref[0] * own + row) & (row < own)
    pair = DEST_TILE // block_rows
    here = encoded_ref[pl.ds(step * pair, pair)].reshape(DEST_TILE, channels)
    picked = dot_nt(jnp.where(pick, 1.0, 0.0).astype(half), here)
    left_ref[...] = jnp.concatenate([attended, picked], axis=0).astype(half)
    grad_qt_s[:, dest] = grad_qt.astype(half)

    @pl.when(step == pl.num_programs(0) - 1)
    def _():
        grad_kvt = grad_kv_s[...].T
        gradst = jnp.concatenate(
            [grad_qt_s[...], (grad_kvt[:HD] * factor).astype(half), grad_kvt[HD:].astype(half)], axis=0
        )
        parts = grads_ref.shape[0]
        weights = dot_nn(gradst, hidden_s[...]).T
        terms = dot_nn(gradst, encoded_ref[...].reshape(nodes, channels)).T
        piece = width // parts
        for part in range(parts):
            weight = weights[part * piece : (part + 1) * piece, :]
            term = terms[part * own : (part + 1) * own, :]
            grads_ref[(part - index_ref[0] + parts) % parts] = jnp.concatenate(
                [
                    weight[:, : 2 * HD],
                    term[:, : 2 * HD],
                    jnp.concatenate([weight[: piece // 2, 2 * HD :], weight[piece // 2 :, 2 * HD :]], axis=1),
                    jnp.concatenate([term[:, 2 * HD :], jnp.zeros((own, HD), full)], axis=1),
                ],
                axis=0,
            ).astype(half)


def attention(index, encoded, w_encoder, w_query, w_key, w_value, received, pairs, parts):
    blocks, block_rows, channels = encoded.shape
    nodes = blocks * block_rows
    width = w_encoder.shape[1]
    own = channels // parts
    left_rows = HD + 2 * own
    rows = HD + own + HD // 2 + own
    return pl.pallas_call(
        attention_kernel,
        grid_spec=pltpu.PrefetchScalarGridSpec(
            num_scalar_prefetch=1,
            grid=(nodes // DEST_TILE,),
            in_specs=[
                whole(blocks, block_rows, channels),
                whole(channels, width),
                pl.BlockSpec((width, 2 * HD), lambda j, m: (0, m[0] // 2)),
                pl.BlockSpec((width, 2 * HD), lambda j, m: (0, m[0] // 2)),
                pl.BlockSpec((width, 2 * HD), lambda j, m: (0, m[0] // 2)),
                whole(*received.shape),
                pl.BlockSpec((nodes, DEST_TILE), lambda j, *_: (0, j)),
            ],
            out_specs=[
                pl.BlockSpec((left_rows, DEST_TILE), lambda j, *_: (0, j)),
                whole(parts, rows, 2 * HD),
            ],
            scratch_shapes=[
                pltpu.VMEM((nodes, width), half),
                pltpu.VMEM((nodes, HD), half),
                pltpu.VMEM((nodes, HD), half),
                pltpu.VMEM((nodes, HD), half),
                pltpu.VMEM((HD, nodes), half),
                pltpu.VMEM((HD, nodes), half),
                pltpu.VMEM((HD, nodes), half),
                pltpu.VMEM((HD, nodes), half),
                pltpu.VMEM((nodes, DEST_TILE), full),
                pltpu.VMEM((nodes, DEST_TILE), full),
                pltpu.VMEM((HD, nodes), half),
                pltpu.VMEM((nodes, 2 * HD), full),
            ],
        ),
        out_shape=[
            jax.ShapeDtypeStruct((left_rows, nodes), half),
            jax.ShapeDtypeStruct((parts, rows, 2 * HD), half),
        ],
        compiler_params=pltpu.CompilerParams(vmem_limit_bytes=WIDE),
        cost_estimate=pl.CostEstimate(
            flops=12 * nodes * nodes * HD, bytes_accessed=2 * nodes * nodes, transcendentals=nodes * nodes
        ),
    )(index, encoded, w_encoder, w_query, w_key, w_value, received, pairs)


def meet_kernel(own, left_ref, cot_ref, out_ref, cot_s, sems):
    nodes, width = cot_ref.shape
    some = nodes // MEET_TILES
    copies = []
    for tile in range(MEET_TILES):
        rows = pl.ds(tile * some, some)
        copies.append(pltpu.make_async_copy(cot_ref.at[rows, :], cot_s.at[rows, :], sems.at[tile]))
        copies[-1].start()
    met = jnp.zeros((left_ref.shape[0], width), full)
    for tile in range(MEET_TILES):
        copies[tile].wait()
        rows = slice(tile * some, (tile + 1) * some)
        met += dot_nn(left_ref[:, rows], cot_s[rows, :])
    parts, rows, columns = out_ref.shape
    piece = width // parts
    spare = rows - HD // 2 - own
    for part in range(parts):
        mine = met[:, part * piece : (part + 1) * piece]
        out_ref[part] = jnp.concatenate(
            [
                jnp.concatenate([mine[: HD // 2], mine[HD // 2 : HD]], axis=1),
                jnp.concatenate([jnp.zeros((own, piece), full), mine[HD : HD + own]], axis=1),
                jnp.zeros((spare, columns), full),
            ],
            axis=0,
        ).astype(half)


def meet(left, all_cot, parts, own):
    rows, nodes = left.shape
    width = all_cot.shape[1]
    out_rows = HD // 2 + 2 * own
    return pl.pallas_call(
        functools.partial(meet_kernel, own),
        grid=(1,),
        in_specs=[whole(rows, nodes), pl.BlockSpec(memory_space=pl.ANY)],
        out_specs=whole(parts, out_rows, 2 * HD),
        out_shape=jax.ShapeDtypeStruct((parts, out_rows, 2 * HD), half),
        scratch_shapes=[pltpu.VMEM((nodes, width), half), pltpu.SemaphoreType.DMA((MEET_TILES,))],
        compiler_params=pltpu.CompilerParams(vmem_limit_bytes=WIDE),
        cost_estimate=pl.CostEstimate(
            flops=2 * rows * nodes * width, bytes_accessed=2 * nodes * width, transcendentals=0
        ),
    )(left, all_cot)


def add_parts(ref):
    total = ref[0].astype(full)
    for part in range(1, ref.shape[0]):
        total += ref[part].astype(full)
    return total


def join_kernel(own, met_ref, swapped_ref, out_ref):
    met = add_parts(met_ref)
    swapped = swapped_ref[...].astype(full)
    half_rows = HD // 2
    last = swapped.shape[0] - own
    joined = jnp.concatenate(
        [swapped[:last], swapped[last:] + met[half_rows : half_rows + own], met[:half_rows]], axis=0
    ).astype(half)
    for part in range(out_ref.shape[0]):
        out_ref[part] = joined


def join(met, swapped, own):
    parts = met.shape[0]
    rows, columns = swapped.shape
    return pl.pallas_call(
        functools.partial(join_kernel, own),
        out_shape=jax.ShapeDtypeStruct((parts, rows + HD // 2, columns), half),
        compiler_params=pltpu.CompilerParams(vmem_limit_bytes=SMALL),
    )(met, swapped)


def bring_kernel(w_query_ref, w_key_ref, w_value_ref, after_ref, out_ref, sems):
    copies = []
    for place, ref in enumerate((w_query_ref, w_key_ref, w_value_ref)):
        copies.append(pltpu.make_async_copy(ref, out_ref.at[place], sems.at[place]))
        copies[-1].start()
    for copy in copies:
        copy.wait()


def bring(w_query, w_key, w_value, after):
    width = w_query.shape[0]
    anywhere = pl.BlockSpec(memory_space=pl.ANY)
    return pl.pallas_call(
        bring_kernel,
        in_specs=[anywhere] * 4,
        out_specs=anywhere,
        out_shape=jax.ShapeDtypeStruct((3, width, width), half),
        scratch_shapes=[pltpu.SemaphoreType.DMA((3,))],
        compiler_params=pltpu.CompilerParams(vmem_limit_bytes=SMALL),
        cost_estimate=pl.CostEstimate(flops=0, bytes_accessed=12 * width * width, transcendentals=0),
    )(w_query, w_key, w_value, after)


def finish_kernel(
    norm, own, index_ref, sums_ref, weights_ref, query_ref, key_ref, value_ref, output_ref, encoder_ref
):
    parts = sums_ref.shape[0]
    edge = HD + own
    last = edge + HD // 2
    high = last + own
    index = index_ref[0]

    def unpack(part):
        piece = sums_ref[(index - part + parts) % parts].astype(full)
        met = sums_ref[part].astype(full)
        value = jnp.concatenate([piece[edge:last, :HD], piece[edge:last, HD:]], axis=0)
        output = jnp.concatenate([met[high:, :HD], met[high:, HD:]], axis=0)
        weights = (piece[:HD, :HD], piece[:HD, HD:], value, output)
        terms = (piece[HD:edge, :HD], piece[HD:edge, HD:], piece[last:high, :HD], met[last:high, HD:])
        return weights, terms

    all_terms = ([], [], [], [])
    for pair in range(parts // 2):
        first, second = unpack(2 * pair), unpack(2 * pair + 1)
        columns = slice(2 * pair * HD, (2 * pair + 2) * HD)
        for place, out in enumerate((query_ref, key_ref, value_ref, output_ref)):
            out[:, columns] = jnp.concatenate([first[0][place], second[0][place]], axis=1) * norm
            all_terms[place].extend((first[1][place], second[1][place]))
    encoder = jnp.concatenate(all_terms[3], axis=1)
    for place in range(3):
        encoder += dot_nt(weights_ref[place], jnp.concatenate(all_terms[place], axis=1).astype(half)).T
    encoder_ref[...] = encoder * norm


def finish(index, sums, weights, norm, own):
    width = weights.shape[1]
    return pl.pallas_call(
        functools.partial(finish_kernel, norm, own),
        grid_spec=pltpu.PrefetchScalarGridSpec(
            num_scalar_prefetch=1,
            grid=(1,),
            in_specs=[whole(*sums.shape), whole(*weights.shape)],
            out_specs=[whole(HD, width)] * 4 + [whole(own, width)],
        ),
        out_shape=[jax.ShapeDtypeStruct((HD, width), full)] * 4 + [jax.ShapeDtypeStruct((own, width), full)],
        compiler_params=pltpu.CompilerParams(vmem_limit_bytes=ROOM),
    )(index, sums, weights)


def exchange(array, axis):
    return lax.all_to_all(array, axis, split_axis=0, concat_axis=0, tiled=True)


def per_device(
    grid_fields,
    cotangent,
    encoder_source,
    encoder_target,
    encoder_count,
    mesh_source,
    mesh_target,
    mesh_count,
    w_encoder,
    w_query,
    w_key,
    w_value,
    w_output,
):
    model_size = lax.axis_size("mp")
    data_size = lax.axis_size("dp")
    model_index = lax.axis_index("mp")
    local_grid = grid_fields[0]
    local_cot = cotangent[0]
    points, channels = local_grid.shape
    node_rows, width = local_cot.shape
    nodes = node_rows * model_size
    own_channels = channels // model_size

    other = lax.ppermute(local_cot, "mp", [(i, i ^ 1) for i in range(model_size)])

    partials = encoder_partials(
        local_grid,
        encoder_source,
        encoder_target,
        encoder_count,
        (model_index * points).reshape(1).astype(jnp.int32),
        w_output,
        local_cot,
    )
    received = exchange(partials, "mp")
    copies, both = collect((model_index % 2).reshape(1).astype(jnp.int32), received, local_cot, other)
    encoded = exchange(copies, "mp")
    lanes = [list(range(first, model_size, 2)) for first in range(2)]
    all_cot = lax.all_gather(both, "mp", axis=0, tiled=True, axis_index_groups=lanes)

    pairs = edge_counts(mesh_source, mesh_target, mesh_count, nodes)
    place = model_index.reshape(1).astype(jnp.int32)
    left, grads = attention(
        place,
        encoded,
        w_encoder,
        w_query,
        w_key,
        w_value,
        received,
        pairs,
        data_size,
    )

    shares = exchange(grads, "dp")
    share = jnp.sum(shares.astype(full), axis=0).astype(half)
    across = [
        (data * model_size + model, data * model_size + (model + data) % model_size)
        for data in range(data_size)
        for model in range(model_size)
    ]
    swapped = lax.ppermute(share, ("dp", "mp"), across)
    met = exchange(meet(left, all_cot, data_size, own_channels), "dp")
    joined = join(met, swapped, own_channels)
    weights = bring(w_query, w_key, w_value, joined)
    sums = exchange(joined, "dp")
    norm = 1.0 / math.sqrt(data_size * nodes)
    return tuple(finish(place, sums, weights, norm, own_channels))


def solution(mesh):
    in_specs = (
        P("dp", "mp", None),
        P("dp", "mp", None),
        P(),
        P(),
        P(),
        P(),
        P(),
        P(),
        P(),
        P(),
        P(),
        P(),
        P(),
    )
    out_specs = (P("mp", None), P("mp", None), P("mp", None), P("mp", None), P("mp", None))
    return jax.shard_map(
        per_device, mesh=mesh, in_specs=in_specs, out_specs=out_specs, check_vma=False
    )
```

time: 205 us -> 163 us (0.80)
  blocking collectives: 46.6 us -> 0 us
  starting transfers between devices: 19.7 us -> 41 us
  Pallas kernels: 70 us -> 53.3 us
  waiting for transfers between devices: 35.7 us -> 44.4 us
  local copies, waits for them, and re-layouts: 13.6 us -> 9.4 us
  other arithmetic: 4.17 us -> 0.07 us
    all_to_all x2 -> x0, blocking collectives: 46.6 us -> none  [the longest x1 24.2 us: spread(): return lax.all_to_all(copies, axis, split_axis=0, concat_axis=0, tiled=True)]
    all_to_all x2 -> x5, starting transfers between devices: 15.2 us -> 37.6 us  [exchange(): return lax.all_to_all(array, axis, split_axis=0, concat_axis=0, tiled=True)]
    pallas_call x1, Pallas kernels: 24.1 us -> 10.5 us  [encoder_partials(): pl.pallas_call(encoder_kernel, grid_spec=pltpu.PrefetchScalarGridSpec(num...]
    pallas_call x1, Pallas kernels: 14.1 us -> 10.6 us  [edge_counts(): pl.pallas_call(edges_kernel, grid_spec=pltpu.PrefetchScalarGridSpec(num_s...]
    pallas_call x2 -> x5, Pallas kernels: 6.28 us -> 9.36 us  [the longest x1 4.23 us: meet(): pl.pallas_call(functools.partial(meet_kernel, own), grid=(1,), in_specs=[...]
    concatenate x2 -> x0, other arithmetic: 2.97 us -> none  [the longest x1 2.08 us: per_device(): jnp.concatenate([lax.dynamic_slice_in_dim(item, first, HD, 1) for item in...]
    all_gather x1, waiting for transfers between devices: 0.01 us -> 2.97 us  [per_device(): lax.all_gather(both, 'mp', axis=0, tiled=True, axis_index_groups=lanes)]
    pallas_call x1, Pallas kernels: 25.5 us -> 22.8 us  [attention(): pl.pallas_call(attention_kernel, grid_spec=pltpu.PrefetchScalarGridSpec(n...]
  transfers between devices with their start and end apart: 5 -> 8, of which waited for: 4 -> 8; matrix products, arithmetic and copies ran while one was open for 3% -> 0% of each run, Pallas kernels for 31% -> 23%
where the time goes in v2:
time: 163 us; the launch traced here: 162 us
  Pallas kernels  53.3 us (33%)
  waiting for transfers between devices  44.4 us (27%)
  starting transfers between devices  41 us (25%)
  between operations  14.1 us (9%)
  local copies, waits for them, and re-layouts  9.4 us (6%)
    all_to_all x5, starting transfers between devices, exchange(): return lax.all_to_all(array, axis, split_axis=0, concat_axis=0, tiled=True)  37.6 us
    all_to_all x5, waiting for transfers between devices, exchange(): return lax.all_to_all(array, axis, split_axis=0, concat_axis=0, tiled=True)  29.6 us
    pallas_call x1, Pallas kernels, attention(): pl.pallas_call(attention_kernel, grid_spec=pltpu.PrefetchScalarGridSpec(n...  22.8 us
    pallas_call x1, Pallas kernels, edge_counts(): pl.pallas_call(edges_kernel, grid_spec=pltpu.PrefetchScalarGridSpec(num_s...  10.6 us
    pallas_call x1, Pallas kernels, encoder_partials(): pl.pallas_call(encoder_kernel, grid_spec=pltpu.PrefetchScalarGridSpec(num...  10.5 us
    unnamed x16, local copies, waits for them, and re-layouts  9.4 us
    ppermute x1, waiting for transfers between devices, per_device(): lax.ppermute(local_cot, 'mp', [(i, i ^ 1) for i in range(model_size)])  6.7 us
    ppermute x1, waiting for transfers between devices, per_device(): swapped = lax.ppermute(share, ('dp', 'mp'), across)  5.09 us
  transfers between devices with their start and end apart: 8, of which 8 were waited for; matrix products, arithmetic and copies ran while one was open for 0% of the time, Pallas kernels for 23%

profile of v2, /device:TPU:1, one launch (start us, length us, event | category | flops | bytes accessed | tf_op | source)
XLA Modules:
  0.0 162.3 jit_solution(184560061780016801)
XLA Ops:
  7.2 0.0 copy-start.6
  7.2 10.5 %shard_map.164 = bf16[16,192,128]{2,1,0:T(8,128)(2,1)} custom-call(s32[16]{0:T(128)} %count_ref.2, s32[1]{0:T(128)} %bitcast.2.base_ref, s32[16,2048]{1,0:T(8,128)} %source_ref.2, s32[16,2048]{1,0:T(8,128)} %target_ref.2, bf16[1024,128]{1,0:T(8,128)(2,1)} %bitcast.8, bf16[1024,1024]{1,0:T(8,128)(2,1)} %w_output_ref.1, bf16[128,1024]{1,0:T(8,128)(2,1)} %bitcast.5), custom_call_target="tpu_custom_call" | custom-call | flops 8589934592 | bytes 262144 | tf_op jit(solution)/shard_map/pallas_call | solution.py:90
  17.7 10.1 %all-to-all-start = ((bf16[16,192,128]{2,1,0:T(8,128)(2,1)}), bf16[16,192,128]{2,1,0:T(8,128)(2,1)S(1)}, u32[]{:S(2)}, u32[]{:S(2)}) async-start(bf16[16,192,128]{2,1,0:T(8,128)(2,1)} %shard_map.164), calls=%async_computation | async-start | bytes 1572864 | tf_op jit(solution)/shard_map/all_to_all | solution.py:515
  27.9 0.0 all-gather.2.cloned.1.call-start
  27.9 0.0 copy-done.6
  27.9 1.4 collective-permute-start
  29.4 6.7 %collective-permute-done.other_ref = bf16[128,1024]{1,0:T(8,128)(2,1)S(1)} collective-permute-done((bf16[128,1024]{1,0:T(8,128)(2,1)S(1)}, bf16[128,1024]{1,0:T(8,128)(2,1)S(1)}, u32[]{:S(2)}, u32[]{:S(2)}) %collective-permute-start) | collective-permute-done | bytes 262176 | tf_op jit(solution)/shard_map/ppermute | solution.py:543
  36.1 12.6 %all-to-all-done.received_ref = bf16[16,192,128]{2,1,0:T(8,128)(2,1)S(1)} async-done(((bf16[16,192,128]{2,1,0:T(8,128)(2,1)}), bf16[16,192,128]{2,1,0:T(8,128)(2,1)S(1)}, u32[]{:S(2)}, u32[]{:S(2)}) %all-to-all-start) | async-done | bytes 786464 | tf_op jit(solution)/shard_map/all_to_all | solution.py:515
  48.7 0.0 copy-start.5
  48.7 1.2 shard_map.165
  49.9 0.0 all-gather.2.cloned.1.call-update
  49.9 5.3 %all-to-all-start.1 = ((bf16[16,128,128]{2,1,0:T(8,128)(2,1)}), bf16[16,128,128]{2,1,0:T(8,128)(2,1)S(1)}, u32[]{:S(2)}, u32[]{:S(2)}) async-start(bf16[16,128,128]{2,1,0:T(8,128)(2,1)} %get-tuple-element.9), calls=%async_computation.1 | async-start | bytes 1048576 | tf_op jit(solution)/shard_map/all_to_all | solution.py:515
  55.2 10.6 %shard_map.166.pairs_ref = bf16[2048,2048]{1,0:T(8,128)(2,1)} custom-call(s32[16]{0:T(128)} %count_ref.3, s32[16,512]{1,0:T(8,128)} %source_ref.3, s32[16,512]{1,0:T(8,128)} %target_ref.3), custom_call_target="tpu_custom_call" | custom-call | flops 8589934592 | bytes 8388608 | tf_op jit(solution)/shard_map/pallas_call | solution.py:183
  65.8 0.0 copy-done.5
  65.8 6.8 %all-to-all-done.1.encoded_ref = bf16[16,128,128]{2,1,0:T(8,128)(2,1)S(1)} async-done(((bf16[16,128,128]{2,1,0:T(8,128)(2,1)}), bf16[16,128,128]{2,1,0:T(8,128)(2,1)S(1)}, u32[]{:S(2)}, u32[]{:S(2)}) %all-to-all-start.1) | async-done | bytes 524320 | tf_op jit(solution)/shard_map/all_to_all | solution.py:515
  72.6 0.0 copy-start.7
  72.6 0.8 copy-done.7
  73.4 22.8 %shard_map.167 = (bf16[80,2048]{1,0:T(8,128)(2,1)}, bf16[16,112,128]{2,1,0:T(8,128)(2,1)}) custom-call(s32[1]{0:T(128)} %bitcast.index_ref, bf16[16,128,128]{2,1,0:T(8,128)(2,1)} %copy-done.7, bf16[128,1024]{1,0:T(8,128)(2,1)} %w_encoder_ref.1, bf16[1024,1024]{1,0:T(8,128)(2,1)} %w_query_ref.3, bf16[1024,1024]{1,0:T(8,128)(2,1)} %w_key_ref.3, ...), custom_call_target="tpu_custom_call" | custom-call | flops 3221225472 | bytes 8388608 | tf_op jit(solution)/shard_map/pallas_call | solution.py:326
  96.2 11.2 %all-to-all-start.3 = ((bf16[16,112,128]{2,1,0:T(8,128)(2,1)}), bf16[16,112,128]{2,1,0:T(8,128)(2,1)S(1)}, u32[]{:S(2)}, u32[]{:S(2)}) async-start(bf16[16,112,128]{2,1,0:T(8,128)(2,1)} %get-tuple-element.12), calls=%async_computation.3 | async-start | bytes 917504 | tf_op jit(solution)/shard_map/all_to_all | solution.py:515
  107.4 3.0 %all-gather.2.cloned.1.call-done.cot_ref = bf16[2048,1024]{1,0:T(8,128)(2,1)} async-done(((bf16[256,1024]{1,0:T(8,128)(2,1)}), bf16[2048,1024]{1,0:T(8,128)(2,1)}) %all-gather.2.cloned.1.call-update) | async-done | bytes 4194320 | tf_op jit(solution)/shard_map/all_gather | solution.py:558
  110.4 4.2 %shard_map.168 = bf16[16,48,128]{2,1,0:T(8,128)(2,1)} custom-call(bf16[80,2048]{1,0:T(8,128)(2,1)} %get-tuple-element.10.left_ref, bf16[2048,1024]{1,0:T(8,128)(2,1)} %all-gather.2.cloned.1.call-done.cot_ref), custom_call_target="tpu_custom_call" | custom-call | flops 335544320 | bytes 4194304 | tf_op jit(solution)/shard_map/pallas_call | solution.py:402
  114.6 0.0 copy-start.2
  114.6 3.2 %all-to-all-done.3 = bf16[16,112,128]{2,1,0:T(8,128)(2,1)S(1)} async-done(((bf16[16,112,128]{2,1,0:T(8,128)(2,1)}), bf16[16,112,128]{2,1,0:T(8,128)(2,1)S(1)}, u32[]{:S(2)}, u32[]{:S(2)}) %all-to-all-start.3) | async-done | bytes 458784 | tf_op jit(solution)/shard_map/all_to_all | solution.py:515
  117.8 4.6 %all-to-all-start.2 = ((bf16[16,48,128]{2,1,0:T(8,128)(2,1)}), bf16[16,48,128]{2,1,0:T(8,128)(2,1)S(1)}, u32[]{:S(2)}, u32[]{:S(2)}) async-start(bf16[16,48,128]{2,1,0:T(8,128)(2,1)} %shard_map.168), calls=%async_computation.2 | async-start | bytes 393216 | tf_op jit(solution)/shard_map/all_to_all | solution.py:515
  122.5 0.1 reduce_sum.12
  122.5 1.9 %collective-permute-start.1 = (bf16[112,128]{1,0:T(8,128)(2,1)S(1)}, bf16[112,128]{1,0:T(8,128)(2,1)S(1)}, u32[]{:S(2)}, u32[]{:S(2)}) collective-permute-start(bf16[112,128]{1,0:T(8,128)(2,1)S(1)} %reduce_sum.12), channel_id=1, source_target_pairs={{0,0},{1,1},{2,2},{3,3},{4,4},{5,5},{6,6},{7,7},{8,8},{9,9},{10,10... | collective-permute-start | bytes 86024 | tf_op jit(solution)/shard_map/ppermute | solution.py:581
  124.5 5.1 %collective-permute-done.1.swapped_ref = bf16[112,128]{1,0:T(8,128)(2,1)S(1)} collective-permute-done((bf16[112,128]{1,0:T(8,128)(2,1)S(1)}, bf16[112,128]{1,0:T(8,128)(2,1)S(1)}, u32[]{:S(2)}, u32[]{:S(2)}) %collective-permute-start.1) | collective-permute-done | bytes 28704 | tf_op jit(solution)/shard_map/ppermute | solution.py:581
  129.6 1.1 all-to-all-done.2.met_ref
  130.7 0.9 shard_map.169.after_ref
  131.6 6.4 %all-to-all-start.4 = ((bf16[16,144,128]{2,1,0:T(8,128)(2,1)}), bf16[16,144,128]{2,1,0:T(8,128)(2,1)S(1)}, u32[]{:S(2)}, u32[]{:S(2)}) async-start(bf16[16,144,128]{2,1,0:T(8,128)(2,1)} %shard_map.169.after_ref), calls=%async_computation.4 | async-start | bytes 1179648 | tf_op jit(solution)/shard_map/all_to_all | solution.py:515
  138.0 0.0 copy-done.2
  138.0 0.0 copy-start.3
  138.0 1.6 copy-done.3
  139.6 0.0 copy-start.4
  139.6 1.6 copy-done.4
  141.2 0.5 shard_map.170.weights_ref
  141.6 0.0 copy-start
  141.6 2.6 %copy-done = bf16[3,1024,1024]{2,1,0:T(8,128)(2,1)} copy-done((bf16[3,1024,1024]{2,1,0:T(8,128)(2,1)}, bf16[3,1024,1024]{2,1,0:T(8,128)(2,1)S(1)}, u32[]{:S(2)}) %copy-start) | copy-done | bytes 6291480
  144.3 5.8 %all-to-all-done.4.sums_ref = bf16[16,144,128]{2,1,0:T(8,128)(2,1)S(1)} async-done(((bf16[16,144,128]{2,1,0:T(8,128)(2,1)}), bf16[16,144,128]{2,1,0:T(8,128)(2,1)S(1)}, u32[]{:S(2)}, u32[]{:S(2)}) %all-to-all-start.4) | async-done | bytes 589856 | tf_op jit(solution)/shard_map/all_to_all | solution.py:515
  150.1 0.0 copy-start.1
  150.1 2.8 %copy-done.1 = bf16[3,1024,1024]{2,1,0:T(8,128)(2,1)S(1)} copy-done((bf16[3,1024,1024]{2,1,0:T(8,128)(2,1)S(1)}, bf16[3,1024,1024]{2,1,0:T(8,128)(2,1)}, u32[]{:S(2)}) %copy-start.1) | copy-done | bytes 6291480
  152.9 2.5 %shard_map.171 = (f32[64,1024]{1,0:T(8,128)}, f32[64,1024]{1,0:T(8,128)}, f32[64,1024]{1,0:T(8,128)}, f32[64,1024]{1,0:T(8,128)}, f32[8,1024]{1,0:T(8,128)}) custom-call(s32[1]{0:T(128)} %bitcast.index_ref, bf16[16,144,128]{2,1,0:T(8,128)(2,1)S(1)} %all-to-all-done.4.sums_ref, bf16[3,1024,1024]{2,1,0:T(8,128)(2,1)S(1)} %copy-done.1), custom_call_target="tpu_custom_call" | custom-call | tf_op jit(solution)/shard_map/pallas_call | solution.py:501
Async XLA Ops:
  7.2 20.8 %copy-start.6 = (bf16[1,128,1024]{2,1,0:T(8,128)(2,1)S(1)}, bf16[1,128,1024]{2,1,0:T(8,128)(2,1)}, u32[]{:S(2)}) copy-start(bf16[1,128,1024]{2,1,0:T(8,128)(2,1)} %param.14) | copy-start | bytes 786436
  17.7 30.9 %all-to-all-start = ((bf16[16,192,128]{2,1,0:T(8,128)(2,1)}), bf16[16,192,128]{2,1,0:T(8,128)(2,1)S(1)}, u32[]{:S(2)}, u32[]{:S(2)}) async-start(bf16[16,192,128]{2,1,0:T(8,128)(2,1)} %shard_map.164), calls=%async_computation | async-start | bytes 1572864 | tf_op jit(solution)/shard_map/all_to_all | solution.py:515
  27.9 82.5 %all-gather.2.cloned.1.call-start = ((), (), s32[]{:S(2)}) async-start(), calls=%async_computation.5 | async-start | bytes 4718592 | tf_op jit(solution)/shard_map/all_gather | solution.py:558
  27.9 8.1 %collective-permute-start = (bf16[128,1024]{1,0:T(8,128)(2,1)S(1)}, bf16[128,1024]{1,0:T(8,128)(2,1)S(1)}, u32[]{:S(2)}, u32[]{:S(2)}) collective-permute-start(bf16[128,1024]{1,0:T(8,128)(2,1)S(1)} %bitcast.6), channel_id=1, source_target_pairs={{0,1},{1,0},{2,3},{3,2},{4,5},{5,4},{6,7},{7,6},{8,9},{9,8},{10,11... | collective-permute-start | bytes 786440 | tf_op jit(solution)/shard_map/ppermute | solution.py:543
  48.7 17.1 %copy-start.5 = (bf16[16,192,128]{2,1,0:T(8,128)(2,1)}, bf16[16,192,128]{2,1,0:T(8,128)(2,1)S(1)}, u32[]{:S(2)}) copy-start(bf16[16,192,128]{2,1,0:T(8,128)(2,1)S(1)} %all-to-all-done.received_ref) | copy-start | bytes 2359300
  49.9 22.7 %all-to-all-start.1 = ((bf16[16,128,128]{2,1,0:T(8,128)(2,1)}), bf16[16,128,128]{2,1,0:T(8,128)(2,1)S(1)}, u32[]{:S(2)}, u32[]{:S(2)}) async-start(bf16[16,128,128]{2,1,0:T(8,128)(2,1)} %get-tuple-element.9), calls=%async_computation.1 | async-start | bytes 1048576 | tf_op jit(solution)/shard_map/all_to_all | solution.py:515
  72.6 0.8 copy-start.7
  96.2 21.6 %all-to-all-start.3 = ((bf16[16,112,128]{2,1,0:T(8,128)(2,1)}), bf16[16,112,128]{2,1,0:T(8,128)(2,1)S(1)}, u32[]{:S(2)}, u32[]{:S(2)}) async-start(bf16[16,112,128]{2,1,0:T(8,128)(2,1)} %get-tuple-element.12), calls=%async_computation.3 | async-start | bytes 917504 | tf_op jit(solution)/shard_map/all_to_all | solution.py:515
  114.6 23.4 %copy-start.2 = (bf16[1024,1024]{1,0:T(8,128)(2,1)S(1)}, bf16[1024,1024]{1,0:T(8,128)(2,1)}, u32[]{:S(2)}) copy-start(bf16[1024,1024]{1,0:T(8,128)(2,1)} %w_query_ref.3) | copy-start | bytes 6291460
  117.8 12.9 %all-to-all-start.2 = ((bf16[16,48,128]{2,1,0:T(8,128)(2,1)}), bf16[16,48,128]{2,1,0:T(8,128)(2,1)S(1)}, u32[]{:S(2)}, u32[]{:S(2)}) async-start(bf16[16,48,128]{2,1,0:T(8,128)(2,1)} %shard_map.168), calls=%async_computation.2 | async-start | bytes 393216 | tf_op jit(solution)/shard_map/all_to_all | solution.py:515
  122.5 7.0 %collective-permute-start.1 = (bf16[112,128]{1,0:T(8,128)(2,1)S(1)}, bf16[112,128]{1,0:T(8,128)(2,1)S(1)}, u32[]{:S(2)}, u32[]{:S(2)}) collective-permute-start(bf16[112,128]{1,0:T(8,128)(2,1)S(1)} %reduce_sum.12), channel_id=1, source_target_pairs={{0,0},{1,1},{2,2},{3,3},{4,4},{5,5},{6,6},{7,7},{8,8},{9,9},{10,10... | collective-permute-start | bytes 86024 | tf_op jit(solution)/shard_map/ppermute | solution.py:581
  131.6 18.5 %all-to-all-start.4 = ((bf16[16,144,128]{2,1,0:T(8,128)(2,1)}), bf16[16,144,128]{2,1,0:T(8,128)(2,1)S(1)}, u32[]{:S(2)}, u32[]{:S(2)}) async-start(bf16[16,144,128]{2,1,0:T(8,128)(2,1)} %shard_map.169.after_ref), calls=%async_computation.4 | async-start | bytes 1179648 | tf_op jit(solution)/shard_map/all_to_all | solution.py:515
  138.0 1.6 copy-start.3
  139.6 1.6 copy-start.4
  141.6 2.7 %copy-start = (bf16[3,1024,1024]{2,1,0:T(8,128)(2,1)}, bf16[3,1024,1024]{2,1,0:T(8,128)(2,1)S(1)}, u32[]{:S(2)}) copy-start(bf16[3,1024,1024]{2,1,0:T(8,128)(2,1)S(1)} %shard_map.170.weights_ref) | copy-start | bytes 18874372
  150.1 2.8 %copy-start.1 = (bf16[3,1024,1024]{2,1,0:T(8,128)(2,1)S(1)}, bf16[3,1024,1024]{2,1,0:T(8,128)(2,1)}, u32[]{:S(2)}) copy-start(bf16[3,1024,1024]{2,1,0:T(8,128)(2,1)} %copy-done) | copy-start | bytes 18874372
Sparse Core Ops, SparseCore 0:
  50.1 60.2 all-gather.1

commit v3 on v2

--- a/solution.py
+++ b/solution.py
@@ -36,8 +36,9 @@
 
 
 def one_hot(rows, index):
-    place = lax.broadcasted_iota(jnp.int32, (rows, index.shape[1]), 0)
-    return jnp.where(place == index, 1.0, 0.0).astype(half)
+    place = lax.broadcasted_iota(jnp.int16, (rows, index.shape[1]), 0)
+    one, zero = jnp.asarray(1.0, half), jnp.asarray(0.0, half)
+    return jnp.where(place == index.astype(jnp.int16), one, zero).astype(jnp.float8_e4m3fn)
 
 
 def encoder_kernel(
@@ -212,8 +213,7 @@
     grads_ref,
     hidden_s,
     query_s,
-    key_s,
-    value_s,
+    key_value_s,
     queryt_s,
     keyt_s,
     valuet_s,
@@ -242,14 +242,13 @@
             hidden_s[rows, :] = hidden
             mixed = dot_nn(hidden, w_head)
             query_s[rows, :] = mixed[:, :HD].astype(half)
-            key_s[rows, :] = mixed[:, HD : 2 * HD].astype(half)
-            value_s[rows, :] = mixed[:, 2 * HD :].astype(half)
+            key_value_s[rows, :] = mixed[:, HD:].astype(half)
             flipped = mixed.T
             queryt_s[:, rows] = (flipped[:HD, :] * factor).astype(half)
             keyt_s[:, rows] = (flipped[HD : 2 * HD, :] * factor).astype(half)
             valuet_s[:, rows] = flipped[2 * HD :, :].astype(half)
         for block in range(blocks):
-            gradt_s[:, block * block_rows : (block + 1) * block_rows] = received_ref[block, block_rows:, :]
+            gradt_s[:, block * block_rows : (block + 1) * block_rows] = received_ref[block]
         grad_kv_s[...] = jnp.zeros_like(grad_kv_s)
 
     dest = pl.ds(pl.multiple_of(step * DEST_TILE, DEST_TILE), DEST_TILE)
@@ -257,20 +256,23 @@
     query, grad = query_s[dest, :], gradt.astype(full).T.astype(half)
     none = jnp.zeros((DEST_TILE, HD), half)
     sides = jnp.concatenate([jnp.concatenate([query, none], axis=1), jnp.concatenate([none, grad], axis=1)], axis=0)
-    total = jnp.zeros((1, DEST_TILE), full)
-    weighted = jnp.zeros((1, DEST_TILE), full)
+    empty = jnp.zeros((HD, DEST_TILE), half)
+    wide = jnp.concatenate([jnp.concatenate([queryt, empty], axis=1), jnp.concatenate([empty, gradt], axis=1)], axis=0)
+    total = jnp.zeros((8, DEST_TILE), full)
+    weighted = jnp.zeros((8, DEST_TILE), full)
     for index in range(nodes // ROW_CHUNK):
         rows = slice(index * ROW_CHUNK, (index + 1) * ROW_CHUNK)
-        score = dot_nn(key_s[rows, :], queryt)
+        both = dot_nn(key_value_s[rows, :], wide)
+        score = both[:, :DEST_TILE]
         times = pairs_ref[rows, :].astype(full)
         expo = jnp.where(times > 0.0, jnp.exp(score), 0.0) * times
-        dattn = dot_nn(value_s[rows, :], gradt)
+        dattn = both[:, DEST_TILE:]
         expo_s[rows, :] = expo
         dattn_s[rows, :] = dattn
-        total += jnp.sum(expo, axis=0, keepdims=True)
-        weighted += jnp.sum(expo * dattn, axis=0, keepdims=True)
-    inverse = 1.0 / total
-    mean_grad = weighted * inverse
+        total += jnp.sum(expo.reshape(-1, 8, DEST_TILE), axis=0)
+        weighted += jnp.sum((expo * dattn).reshape(-1, 8, DEST_TILE), axis=0)
+    inverse = 1.0 / jnp.sum(total, axis=0, keepdims=True)
+    mean_grad = jnp.sum(weighted, axis=0, keepdims=True) * inverse
     attended = jnp.zeros((HD, DEST_TILE), full)
     grad_qt = jnp.zeros((HD, DEST_TILE), full)
     for index in range(nodes // ROW_CHUNK):
@@ -334,7 +336,7 @@
                 pl.BlockSpec((width, 2 * HD), lambda j, m: (0, m[0] // 2)),
                 pl.BlockSpec((width, 2 * HD), lambda j, m: (0, m[0] // 2)),
                 pl.BlockSpec((width, 2 * HD), lambda j, m: (0, m[0] // 2)),
-                whole(*received.shape),
+                pl.BlockSpec((blocks, HD, block_rows), lambda j, *_: (0, block_rows // HD, 0)),
                 pl.BlockSpec((nodes, DEST_TILE), lambda j, *_: (0, j)),
             ],
             out_specs=[
@@ -344,8 +346,7 @@
             scratch_shapes=[
                 pltpu.VMEM((nodes, width), half),
                 pltpu.VMEM((nodes, HD), half),
-                pltpu.VMEM((nodes, HD), half),
-                pltpu.VMEM((nodes, HD), half),
+                pltpu.VMEM((nodes, 2 * HD), half),
                 pltpu.VMEM((HD, nodes), half),
                 pltpu.VMEM((HD, nodes), half),
                 pltpu.VMEM((HD, nodes), half),

time: 163 us -> 160 us (0.982)
  Pallas kernels: 53.3 us -> 47.4 us
  waiting for transfers between devices: 44.4 us -> 46.9 us
    pallas_call x1, Pallas kernels: 10.6 us -> 7.73 us  [edge_counts(): pl.pallas_call(edges_kernel, grid_spec=pltpu.PrefetchScalarGridSpec(num_s...]
    pallas_call x1, Pallas kernels: 10.5 us -> 7.93 us  [encoder_partials(): pl.pallas_call(encoder_kernel, grid_spec=pltpu.PrefetchScalarGridSpec(num...]
    all_to_all x5, waiting for transfers between devices: 29.6 us -> 32 us  [exchange(): return lax.all_to_all(array, axis, split_axis=0, concat_axis=0, tiled=True)]
  transfers between devices with their start and end apart: 8 -> 8, of which waited for: 8 -> 8; matrix products, arithmetic and copies ran while one was open for 0% -> 0% of each run, Pallas kernels for 23% -> 22%
where the time goes in v3:
time: 160 us; the launch traced here: 159 us
  Pallas kernels  47.4 us (30%)
  waiting for transfers between devices  46.9 us (29%)
  starting transfers between devices  41.5 us (26%)
  between operations  14.1 us (9%)
  local copies, waits for them, and re-layouts  9.4 us (6%)
    all_to_all x5, starting transfers between devices, exchange(): return lax.all_to_all(array, axis, split_axis=0, concat_axis=0, tiled=True)  37.7 us
    all_to_all x5, waiting for transfers between devices, exchange(): return lax.all_to_all(array, axis, split_axis=0, concat_axis=0, tiled=True)  32 us
    pallas_call x1, Pallas kernels, attention(): pl.pallas_call(attention_kernel, grid_spec=pltpu.PrefetchScalarGridSpec(n...  22.4 us
    unnamed x16, local copies, waits for them, and re-layouts  9.4 us
    pallas_call x1, Pallas kernels, encoder_partials(): pl.pallas_call(encoder_kernel, grid_spec=pltpu.PrefetchScalarGridSpec(num...  7.93 us
    pallas_call x1, Pallas kernels, edge_counts(): pl.pallas_call(edges_kernel, grid_spec=pltpu.PrefetchScalarGridSpec(num_s...  7.73 us
    ppermute x1, waiting for transfers between devices, per_device(): lax.ppermute(local_cot, 'mp', [(i, i ^ 1) for i in range(model_size)])  6.7 us
    ppermute x1, waiting for transfers between devices, per_device(): swapped = lax.ppermute(share, ('dp', 'mp'), across)  4.72 us
  transfers between devices with their start and end apart: 8, of which 8 were waited for; matrix products, arithmetic and copies ran while one was open for 0% of the time, Pallas kernels for 22%

profile of v3, /device:TPU:1, one launch (start us, length us, event | category | flops | bytes accessed | tf_op | source)
XLA Modules:
  0.0 159.4 jit_solution(14843720133559298222)
XLA Ops:
  7.2 0.0 copy-start.6
  7.2 7.9 %shard_map.164 = bf16[16,192,128]{2,1,0:T(8,128)(2,1)} custom-call(s32[16]{0:T(128)} %count_ref.2, s32[1]{0:T(128)} %bitcast.2.base_ref, s32[16,2048]{1,0:T(8,128)} %source_ref.2, s32[16,2048]{1,0:T(8,128)} %target_ref.2, bf16[1024,128]{1,0:T(8,128)(2,1)} %bitcast.8, bf16[1024,1024]{1,0:T(8,128)(2,1)} %w_output_ref.1, bf16[128,1024]{1,0:T(8,128)(2,1)} %bitcast.5), custom_call_target="tpu_custom_call" | custom-call | flops 8589934592 | bytes 262144 | tf_op jit(solution)/shard_map/pallas_call | solution.py:91
  15.1 10.1 %all-to-all-start = ((bf16[16,192,128]{2,1,0:T(8,128)(2,1)}), bf16[16,192,128]{2,1,0:T(8,128)(2,1)S(1)}, u32[]{:S(2)}, u32[]{:S(2)}) async-start(bf16[16,192,128]{2,1,0:T(8,128)(2,1)} %shard_map.164), calls=%async_computation | async-start | bytes 1572864 | tf_op jit(solution)/shard_map/all_to_all | solution.py:516
  25.3 0.0 all-gather.2.cloned.1.call-start
  25.3 0.0 copy-done.6
  25.3 1.4 collective-permute-start
  26.8 6.7 %collective-permute-done.other_ref = bf16[128,1024]{1,0:T(8,128)(2,1)S(1)} collective-permute-done((bf16[128,1024]{1,0:T(8,128)(2,1)S(1)}, bf16[128,1024]{1,0:T(8,128)(2,1)S(1)}, u32[]{:S(2)}, u32[]{:S(2)}) %collective-permute-start) | collective-permute-done | bytes 262176 | tf_op jit(solution)/shard_map/ppermute | solution.py:544
  33.5 12.6 %all-to-all-done.received_ref = bf16[16,192,128]{2,1,0:T(8,128)(2,1)S(1)} async-done(((bf16[16,192,128]{2,1,0:T(8,128)(2,1)}), bf16[16,192,128]{2,1,0:T(8,128)(2,1)S(1)}, u32[]{:S(2)}, u32[]{:S(2)}) %all-to-all-start) | async-done | bytes 786464 | tf_op jit(solution)/shard_map/all_to_all | solution.py:516
  46.1 0.0 copy-start.5
  46.1 1.2 shard_map.165
  47.3 0.0 all-gather.2.cloned.1.call-update
  47.3 5.3 %all-to-all-start.1 = ((bf16[16,128,128]{2,1,0:T(8,128)(2,1)}), bf16[16,128,128]{2,1,0:T(8,128)(2,1)S(1)}, u32[]{:S(2)}, u32[]{:S(2)}) async-start(bf16[16,128,128]{2,1,0:T(8,128)(2,1)} %get-tuple-element.9), calls=%async_computation.1 | async-start | bytes 1048576 | tf_op jit(solution)/shard_map/all_to_all | solution.py:516
  52.6 7.7 %shard_map.166.pairs_ref = bf16[2048,2048]{1,0:T(8,128)(2,1)} custom-call(s32[16]{0:T(128)} %count_ref.3, s32[16,512]{1,0:T(8,128)} %source_ref.3, s32[16,512]{1,0:T(8,128)} %target_ref.3), custom_call_target="tpu_custom_call" | custom-call | flops 8589934592 | bytes 8388608 | tf_op jit(solution)/shard_map/pallas_call | solution.py:184
  60.3 0.0 copy-done.5
  60.3 9.7 %all-to-all-done.1.encoded_ref = bf16[16,128,128]{2,1,0:T(8,128)(2,1)S(1)} async-done(((bf16[16,128,128]{2,1,0:T(8,128)(2,1)}), bf16[16,128,128]{2,1,0:T(8,128)(2,1)S(1)}, u32[]{:S(2)}, u32[]{:S(2)}) %all-to-all-start.1) | async-done | bytes 524320 | tf_op jit(solution)/shard_map/all_to_all | solution.py:516
  70.0 0.0 copy-start.7
  70.0 0.8 copy-done.7
  70.8 22.4 %shard_map.167 = (bf16[80,2048]{1,0:T(8,128)(2,1)}, bf16[16,112,128]{2,1,0:T(8,128)(2,1)}) custom-call(s32[1]{0:T(128)} %bitcast.index_ref, bf16[16,128,128]{2,1,0:T(8,128)(2,1)} %copy-done.7, bf16[128,1024]{1,0:T(8,128)(2,1)} %w_encoder_ref.1, bf16[1024,1024]{1,0:T(8,128)(2,1)} %w_query_ref.3, bf16[1024,1024]{1,0:T(8,128)(2,1)} %w_key_ref.3, ...), custom_call_target="tpu_custom_call" | custom-call | flops 3221225472 | bytes 8388608 | tf_op jit(solution)/shard_map/pallas_call | solution.py:328
  93.2 11.2 %all-to-all-start.3 = ((bf16[16,112,128]{2,1,0:T(8,128)(2,1)}), bf16[16,112,128]{2,1,0:T(8,128)(2,1)S(1)}, u32[]{:S(2)}, u32[]{:S(2)}) async-start(bf16[16,112,128]{2,1,0:T(8,128)(2,1)} %get-tuple-element.12), calls=%async_computation.3 | async-start | bytes 917504 | tf_op jit(solution)/shard_map/all_to_all | solution.py:516
  104.4 3.4 %all-gather.2.cloned.1.call-done.cot_ref = bf16[2048,1024]{1,0:T(8,128)(2,1)} async-done(((bf16[256,1024]{1,0:T(8,128)(2,1)}), bf16[2048,1024]{1,0:T(8,128)(2,1)}) %all-gather.2.cloned.1.call-update) | async-done | bytes 4194320 | tf_op jit(solution)/shard_map/all_gather | solution.py:559
  107.8 4.2 %shard_map.168 = bf16[16,48,128]{2,1,0:T(8,128)(2,1)} custom-call(bf16[80,2048]{1,0:T(8,128)(2,1)} %get-tuple-element.10.left_ref, bf16[2048,1024]{1,0:T(8,128)(2,1)} %all-gather.2.cloned.1.call-done.cot_ref), custom_call_target="tpu_custom_call" | custom-call | flops 335544320 | bytes 4194304 | tf_op jit(solution)/shard_map/pallas_call | solution.py:403
  112.0 0.0 copy-start.2
  112.0 2.8 %all-to-all-done.3 = bf16[16,112,128]{2,1,0:T(8,128)(2,1)S(1)} async-done(((bf16[16,112,128]{2,1,0:T(8,128)(2,1)}), bf16[16,112,128]{2,1,0:T(8,128)(2,1)S(1)}, u32[]{:S(2)}, u32[]{:S(2)}) %all-to-all-start.3) | async-done | bytes 458784 | tf_op jit(solution)/shard_map/all_to_all | solution.py:516
  114.8 4.6 %all-to-all-start.2 = ((bf16[16,48,128]{2,1,0:T(8,128)(2,1)}), bf16[16,48,128]{2,1,0:T(8,128)(2,1)S(1)}, u32[]{:S(2)}, u32[]{:S(2)}) async-start(bf16[16,48,128]{2,1,0:T(8,128)(2,1)} %shard_map.168), calls=%async_computation.2 | async-start | bytes 393216 | tf_op jit(solution)/shard_map/all_to_all | solution.py:516
  119.5 0.1 reduce_sum.12
  119.5 2.3 %collective-permute-start.1 = (bf16[112,128]{1,0:T(8,128)(2,1)S(1)}, bf16[112,128]{1,0:T(8,128)(2,1)S(1)}, u32[]{:S(2)}, u32[]{:S(2)}) collective-permute-start(bf16[112,128]{1,0:T(8,128)(2,1)S(1)} %reduce_sum.12), channel_id=1, source_target_pairs={{0,0},{1,1},{2,2},{3,3},{4,4},{5,5},{6,6},{7,7},{8,8},{9,9},{10,10... | collective-permute-start | bytes 86024 | tf_op jit(solution)/shard_map/ppermute | solution.py:582
  121.8 4.7 %collective-permute-done.1.swapped_ref = bf16[112,128]{1,0:T(8,128)(2,1)S(1)} collective-permute-done((bf16[112,128]{1,0:T(8,128)(2,1)S(1)}, bf16[112,128]{1,0:T(8,128)(2,1)S(1)}, u32[]{:S(2)}, u32[]{:S(2)}) %collective-permute-start.1) | collective-permute-done | bytes 28704 | tf_op jit(solution)/shard_map/ppermute | solution.py:582
  126.5 1.1 all-to-all-done.2.met_ref
  127.7 0.9 shard_map.169.after_ref
  128.6 6.5 %all-to-all-start.4 = ((bf16[16,144,128]{2,1,0:T(8,128)(2,1)}), bf16[16,144,128]{2,1,0:T(8,128)(2,1)S(1)}, u32[]{:S(2)}, u32[]{:S(2)}) async-start(bf16[16,144,128]{2,1,0:T(8,128)(2,1)} %shard_map.169.after_ref), calls=%async_computation.4 | async-start | bytes 1179648 | tf_op jit(solution)/shard_map/all_to_all | solution.py:516
  135.1 0.0 copy-done.2
  135.1 0.0 copy-start.3
  135.1 1.6 copy-done.3
  136.7 0.0 copy-start.4
  136.7 1.6 copy-done.4
  138.3 0.5 shard_map.170.weights_ref
  138.8 0.0 copy-start
  138.8 2.6 %copy-done = bf16[3,1024,1024]{2,1,0:T(8,128)(2,1)} copy-done((bf16[3,1024,1024]{2,1,0:T(8,128)(2,1)}, bf16[3,1024,1024]{2,1,0:T(8,128)(2,1)S(1)}, u32[]{:S(2)}) %copy-start) | copy-done | bytes 6291480
  141.4 5.8 %all-to-all-done.4.sums_ref = bf16[16,144,128]{2,1,0:T(8,128)(2,1)S(1)} async-done(((bf16[16,144,128]{2,1,0:T(8,128)(2,1)}), bf16[16,144,128]{2,1,0:T(8,128)(2,1)S(1)}, u32[]{:S(2)}, u32[]{:S(2)}) %all-to-all-start.4) | async-done | bytes 589856 | tf_op jit(solution)/shard_map/all_to_all | solution.py:516
  147.2 0.0 copy-start.1
  147.2 2.8 %copy-done.1 = bf16[3,1024,1024]{2,1,0:T(8,128)(2,1)S(1)} copy-done((bf16[3,1024,1024]{2,1,0:T(8,128)(2,1)S(1)}, bf16[3,1024,1024]{2,1,0:T(8,128)(2,1)}, u32[]{:S(2)}) %copy-start.1) | copy-done | bytes 6291480
  150.0 2.5 %shard_map.171 = (f32[64,1024]{1,0:T(8,128)}, f32[64,1024]{1,0:T(8,128)}, f32[64,1024]{1,0:T(8,128)}, f32[64,1024]{1,0:T(8,128)}, f32[8,1024]{1,0:T(8,128)}) custom-call(s32[1]{0:T(128)} %bitcast.index_ref, bf16[16,144,128]{2,1,0:T(8,128)(2,1)S(1)} %all-to-all-done.4.sums_ref, bf16[3,1024,1024]{2,1,0:T(8,128)(2,1)S(1)} %copy-done.1), custom_call_target="tpu_custom_call" | custom-call | tf_op jit(solution)/shard_map/pallas_call | solution.py:502
Async XLA Ops:
  7.2 18.2 %copy-start.6 = (bf16[1,128,1024]{2,1,0:T(8,128)(2,1)S(1)}, bf16[1,128,1024]{2,1,0:T(8,128)(2,1)}, u32[]{:S(2)}) copy-start(bf16[1,128,1024]{2,1,0:T(8,128)(2,1)} %param.14) | copy-start | bytes 786436
  15.1 30.9 %all-to-all-start = ((bf16[16,192,128]{2,1,0:T(8,128)(2,1)}), bf16[16,192,128]{2,1,0:T(8,128)(2,1)S(1)}, u32[]{:S(2)}, u32[]{:S(2)}) async-start(bf16[16,192,128]{2,1,0:T(8,128)(2,1)} %shard_map.164), calls=%async_computation | async-start | bytes 1572864 | tf_op jit(solution)/shard_map/all_to_all | solution.py:516
  25.3 82.5 %all-gather.2.cloned.1.call-start = ((), (), s32[]{:S(2)}) async-start(), calls=%async_computation.5 | async-start | bytes 4718592 | tf_op jit(solution)/shard_map/all_gather | solution.py:559
  25.3 8.1 %collective-permute-start = (bf16[128,1024]{1,0:T(8,128)(2,1)S(1)}, bf16[128,1024]{1,0:T(8,128)(2,1)S(1)}, u32[]{:S(2)}, u32[]{:S(2)}) collective-permute-start(bf16[128,1024]{1,0:T(8,128)(2,1)S(1)} %bitcast.6), channel_id=1, source_target_pairs={{0,1},{1,0},{2,3},{3,2},{4,5},{5,4},{6,7},{7,6},{8,9},{9,8},{10,11... | collective-permute-start | bytes 786440 | tf_op jit(solution)/shard_map/ppermute | solution.py:544
  46.1 14.3 %copy-start.5 = (bf16[16,192,128]{2,1,0:T(8,128)(2,1)}, bf16[16,192,128]{2,1,0:T(8,128)(2,1)S(1)}, u32[]{:S(2)}) copy-start(bf16[16,192,128]{2,1,0:T(8,128)(2,1)S(1)} %all-to-all-done.received_ref) | copy-start | bytes 2359300
  47.3 22.7 %all-to-all-start.1 = ((bf16[16,128,128]{2,1,0:T(8,128)(2,1)}), bf16[16,128,128]{2,1,0:T(8,128)(2,1)S(1)}, u32[]{:S(2)}, u32[]{:S(2)}) async-start(bf16[16,128,128]{2,1,0:T(8,128)(2,1)} %get-tuple-element.9), calls=%async_computation.1 | async-start | bytes 1048576 | tf_op jit(solution)/shard_map/all_to_all | solution.py:516
  70.0 0.8 copy-start.7
  93.2 21.6 %all-to-all-start.3 = ((bf16[16,112,128]{2,1,0:T(8,128)(2,1)}), bf16[16,112,128]{2,1,0:T(8,128)(2,1)S(1)}, u32[]{:S(2)}, u32[]{:S(2)}) async-start(bf16[16,112,128]{2,1,0:T(8,128)(2,1)} %get-tuple-element.12), calls=%async_computation.3 | async-start | bytes 917504 | tf_op jit(solution)/shard_map/all_to_all | solution.py:516
  112.0 23.1 %copy-start.2 = (bf16[1024,1024]{1,0:T(8,128)(2,1)S(1)}, bf16[1024,1024]{1,0:T(8,128)(2,1)}, u32[]{:S(2)}) copy-start(bf16[1024,1024]{1,0:T(8,128)(2,1)} %w_query_ref.3) | copy-start | bytes 6291460
  114.8 12.9 %all-to-all-start.2 = ((bf16[16,48,128]{2,1,0:T(8,128)(2,1)}), bf16[16,48,128]{2,1,0:T(8,128)(2,1)S(1)}, u32[]{:S(2)}, u32[]{:S(2)}) async-start(bf16[16,48,128]{2,1,0:T(8,128)(2,1)} %shard_map.168), calls=%async_computation.2 | async-start | bytes 393216 | tf_op jit(solution)/shard_map/all_to_all | solution.py:516
  119.5 7.0 %collective-permute-start.1 = (bf16[112,128]{1,0:T(8,128)(2,1)S(1)}, bf16[112,128]{1,0:T(8,128)(2,1)S(1)}, u32[]{:S(2)}, u32[]{:S(2)}) collective-permute-start(bf16[112,128]{1,0:T(8,128)(2,1)S(1)} %reduce_sum.12), channel_id=1, source_target_pairs={{0,0},{1,1},{2,2},{3,3},{4,4},{5,5},{6,6},{7,7},{8,8},{9,9},{10,10... | collective-permute-start | bytes 86024 | tf_op jit(solution)/shard_map/ppermute | solution.py:582
  128.6 18.7 %all-to-all-start.4 = ((bf16[16,144,128]{2,1,0:T(8,128)(2,1)}), bf16[16,144,128]{2,1,0:T(8,128)(2,1)S(1)}, u32[]{:S(2)}, u32[]{:S(2)}) async-start(bf16[16,144,128]{2,1,0:T(8,128)(2,1)} %shard_map.169.after_ref), calls=%async_computation.4 | async-start | bytes 1179648 | tf_op jit(solution)/shard_map/all_to_all | solution.py:516
  135.1 1.6 %copy-start.3 = (bf16[1024,1024]{1,0:T(8,128)(2,1)S(1)}, bf16[1024,1024]{1,0:T(8,128)(2,1)}, u32[]{:S(2)}) copy-start(bf16[1024,1024]{1,0:T(8,128)(2,1)} %w_key_ref.3) | copy-start | bytes 6291460
  136.7 1.6 copy-start.4
  138.8 2.7 %copy-start = (bf16[3,1024,1024]{2,1,0:T(8,128)(2,1)}, bf16[3,1024,1024]{2,1,0:T(8,128)(2,1)S(1)}, u32[]{:S(2)}) copy-start(bf16[3,1024,1024]{2,1,0:T(8,128)(2,1)S(1)} %shard_map.170.weights_ref) | copy-start | bytes 18874372
  147.2 2.8 %copy-start.1 = (bf16[3,1024,1024]{2,1,0:T(8,128)(2,1)S(1)}, bf16[3,1024,1024]{2,1,0:T(8,128)(2,1)}, u32[]{:S(2)}) copy-start(bf16[3,1024,1024]{2,1,0:T(8,128)(2,1)} %copy-done) | copy-start | bytes 18874372
Sparse Core Ops, SparseCore 0:
  47.5 60.2 all-gather.1

commit v4 on v3

--- a/solution.py
+++ b/solution.py
@@ -18,7 +18,6 @@
 MEET_TILES = 4
 WIDE = 60 * 1024 * 1024
 SMALL = 12 * 1024 * 1024
-ROOM = 24 * 1024 * 1024
 half = jnp.bfloat16
 full = jnp.float32
 
@@ -156,7 +155,31 @@
     )(odd, received, own, other)
 
 
-def edges_kernel(count_ref, source_ref, target_ref, out_ref):
+def split(value):
+    high = value.astype(half)
+    return high, (value - high.astype(full)).astype(half)
+
+
+def edges_kernel(
+    count_ref,
+    index_ref,
+    source_ref,
+    target_ref,
+    w_encoder_ref,
+    w_query_ref,
+    w_key_ref,
+    w_value_ref,
+    out_ref,
+    folded_ref,
+):
+    @pl.when(pl.program_id(0) == 0)
+    def _():
+        odd = index_ref[0] % 2 == 1
+        w_head = jnp.concatenate(
+            [jnp.where(odd, ref[:, HD:], ref[:, :HD]) for ref in (w_query_ref, w_key_ref, w_value_ref)], axis=1
+        )
+        folded_ref[...] = jnp.concatenate(split(dot_nn(w_encoder_ref[...], w_head)), axis=0)
+
     slots = source_ref.shape[1]
     nodes, columns_here = out_ref.shape
     blocks = columns_here // BLOCK
@@ -178,40 +201,42 @@
             ).astype(half)
 
 
-def edge_counts(source, target, count, nodes):
+def edge_counts(source, target, count, index, w_encoder, w_query, w_key, w_value, nodes):
     blocks, slots = source.shape
+    channels, width = w_encoder.shape
     some = EDGE_BLOCKS
+    head = pl.BlockSpec((width, 2 * HD), lambda b, c, m: (0, m[0] // 2))
     return pl.pallas_call(
         edges_kernel,
         grid_spec=pltpu.PrefetchScalarGridSpec(
-            num_scalar_prefetch=1,
+            num_scalar_prefetch=2,
             grid=(blocks // some,),
-            in_specs=[
-                whole(blocks, slots),
-                whole(blocks, slots),
-            ],
-            out_specs=pl.BlockSpec((nodes, some * BLOCK), lambda b, *_: (0, b)),
-        ),
-        out_shape=jax.ShapeDtypeStruct((nodes, nodes), half),
+            in_specs=[whole(blocks, slots), whole(blocks, slots), whole(channels, width), head, head, head],
+            out_specs=[
+                pl.BlockSpec((nodes, some * BLOCK), lambda b, *_: (0, b)),
+                whole(2 * channels, 3 * HD),
+            ],
+        ),
+        out_shape=[
+            jax.ShapeDtypeStruct((nodes, nodes), half),
+            jax.ShapeDtypeStruct((2 * channels, 3 * HD), half),
+        ],
         compiler_params=pltpu.CompilerParams(vmem_limit_bytes=WIDE),
         cost_estimate=pl.CostEstimate(
             flops=2 * nodes * blocks * slots * BLOCK * 2, bytes_accessed=2 * nodes * nodes, transcendentals=0
         ),
-    )(count, source, target)
+    )(count, index, source, target, w_encoder, w_query, w_key, w_value)
 
 
 def attention_kernel(
     index_ref,
     encoded_ref,
     w_encoder_ref,
-    w_query_ref,
-    w_key_ref,
-    w_value_ref,
+    folded_ref,
     received_ref,
     pairs_ref,
     left_ref,
     grads_ref,
-    hidden_s,
     query_s,
     key_value_s,
     queryt_s,
@@ -232,15 +257,9 @@
     @pl.when(step == 0)
     def _():
         encoded = encoded_ref[...].reshape(nodes, channels)
-        odd = index_ref[0] % 2 == 1
-        w_head = jnp.concatenate(
-            [jnp.where(odd, ref[:, HD:], ref[:, :HD]) for ref in (w_query_ref, w_key_ref, w_value_ref)], axis=1
-        )
         for index in range(nodes // ROW_CHUNK):
             rows = slice(index * ROW_CHUNK, (index + 1) * ROW_CHUNK)
-            hidden = dot_nn(encoded[rows], w_encoder_ref[...]).astype(half)
-            hidden_s[rows, :] = hidden
-            mixed = dot_nn(hidden, w_head)
+            mixed = dot_nn(jnp.concatenate([encoded[rows], encoded[rows]], axis=1), folded_ref[...])
             query_s[rows, :] = mixed[:, :HD].astype(half)
             key_value_s[rows, :] = mixed[:, HD:].astype(half)
             flipped = mixed.T
@@ -301,8 +320,12 @@
             [grad_qt_s[...], (grad_kvt[:HD] * factor).astype(half), grad_kvt[HD:].astype(half)], axis=0
         )
         parts = grads_ref.shape[0]
-        weights = dot_nn(gradst, hidden_s[...]).T
-        terms = dot_nn(gradst, encoded_ref[...].reshape(nodes, channels)).T
+        terms = dot_nn(gradst, encoded_ref[...].reshape(nodes, channels))
+        w_encoder = w_encoder_ref[...]
+        weights = dot_nn(
+            jnp.concatenate(split(terms), axis=1), jnp.concatenate([w_encoder, w_encoder], axis=0)
+        ).T
+        terms = terms.T
         piece = width // parts
         for part in range(parts):
             weight = weights[part * piece : (part + 1) * piece, :]
@@ -318,7 +341,7 @@
             ).astype(half)
 
 
-def attention(index, encoded, w_encoder, w_query, w_key, w_value, received, pairs, parts):
+def attention(index, encoded, w_encoder, folded, received, pairs, parts):
     blocks, block_rows, channels = encoded.shape
     nodes = blocks * block_rows
     width = w_encoder.shape[1]
@@ -333,9 +356,7 @@
             in_specs=[
                 whole(blocks, block_rows, channels),
                 whole(channels, width),
-                pl.BlockSpec((width, 2 * HD), lambda j, m: (0, m[0] // 2)),
-                pl.BlockSpec((width, 2 * HD), lambda j, m: (0, m[0] // 2)),
-                pl.BlockSpec((width, 2 * HD), lambda j, m: (0, m[0] // 2)),
+                whole(*folded.shape),
                 pl.BlockSpec((blocks, HD, block_rows), lambda j, *_: (0, block_rows // HD, 0)),
                 pl.BlockSpec((nodes, DEST_TILE), lambda j, *_: (0, j)),
             ],
@@ -344,7 +365,6 @@
                 whole(parts, rows, 2 * HD),
             ],
             scratch_shapes=[
-                pltpu.VMEM((nodes, width), half),
                 pltpu.VMEM((nodes, HD), half),
                 pltpu.VMEM((nodes, 2 * HD), half),
                 pltpu.VMEM((HD, nodes), half),
@@ -365,18 +385,21 @@
         cost_estimate=pl.CostEstimate(
             flops=12 * nodes * nodes * HD, bytes_accessed=2 * nodes * nodes, transcendentals=nodes * nodes
         ),
-    )(index, encoded, w_encoder, w_query, w_key, w_value, received, pairs)
-
-
-def meet_kernel(own, left_ref, cot_ref, out_ref, cot_s, sems):
+    )(index, encoded, w_encoder, folded, received, pairs)
+
+
+def meet_kernel(own, left_any, cot_ref, out_ref, left_ref, cot_s, sems):
     nodes, width = cot_ref.shape
     some = nodes // MEET_TILES
+    first = pltpu.make_async_copy(left_any, left_ref, sems.at[MEET_TILES])
+    first.start()
     copies = []
     for tile in range(MEET_TILES):
         rows = pl.ds(tile * some, some)
         copies.append(pltpu.make_async_copy(cot_ref.at[rows, :], cot_s.at[rows, :], sems.at[tile]))
         copies[-1].start()
     met = jnp.zeros((left_ref.shape[0], width), full)
+    first.wait()
     for tile in range(MEET_TILES):
         copies[tile].wait()
         rows = slice(tile * some, (tile + 1) * some)
@@ -403,10 +426,14 @@
     return pl.pallas_call(
         functools.partial(meet_kernel, own),
         grid=(1,),
-        in_specs=[whole(rows, nodes), pl.BlockSpec(memory_space=pl.ANY)],
+        in_specs=[pl.BlockSpec(memory_space=pl.ANY)] * 2,
         out_specs=whole(parts, out_rows, 2 * HD),
         out_shape=jax.ShapeDtypeStruct((parts, out_rows, 2 * HD), half),
-        scratch_shapes=[pltpu.VMEM((nodes, width), half), pltpu.SemaphoreType.DMA((MEET_TILES,))],
+        scratch_shapes=[
+            pltpu.VMEM((rows, nodes), half),
+            pltpu.VMEM((nodes, width), half),
+            pltpu.SemaphoreType.DMA((MEET_TILES + 1,)),
+        ],
         compiler_params=pltpu.CompilerParams(vmem_limit_bytes=WIDE),
         cost_estimate=pl.CostEstimate(
             flops=2 * rows * nodes * width, bytes_accessed=2 * nodes * width, transcendentals=0
@@ -443,32 +470,26 @@
     )(met, swapped)
 
 
-def bring_kernel(w_query_ref, w_key_ref, w_value_ref, after_ref, out_ref, sems):
+def finish_kernel(
+    norm,
+    own,
+    index_ref,
+    sums_ref,
+    w_query_ref,
+    w_key_ref,
+    w_value_ref,
+    query_ref,
+    key_ref,
+    value_ref,
+    output_ref,
+    encoder_ref,
+    weights_ref,
+    sems,
+):
     copies = []
     for place, ref in enumerate((w_query_ref, w_key_ref, w_value_ref)):
-        copies.append(pltpu.make_async_copy(ref, out_ref.at[place], sems.at[place]))
+        copies.append(pltpu.make_async_copy(ref, weights_ref.at[place], sems.at[place]))
         copies[-1].start()
-    for copy in copies:
-        copy.wait()
-
-
-def bring(w_query, w_key, w_value, after):
-    width = w_query.shape[0]
-    anywhere = pl.BlockSpec(memory_space=pl.ANY)
-    return pl.pallas_call(
-        bring_kernel,
-        in_specs=[anywhere] * 4,
-        out_specs=anywhere,
-        out_shape=jax.ShapeDtypeStruct((3, width, width), half),
-        scratch_shapes=[pltpu.SemaphoreType.DMA((3,))],
-        compiler_params=pltpu.CompilerParams(vmem_limit_bytes=SMALL),
-        cost_estimate=pl.CostEstimate(flops=0, bytes_accessed=12 * width * width, transcendentals=0),
-    )(w_query, w_key, w_value, after)
-
-
-def finish_kernel(
-    norm, own, index_ref, sums_ref, weights_ref, query_ref, key_ref, value_ref, output_ref, encoder_ref
-):
     parts = sums_ref.shape[0]
     edge = HD + own
     last = edge + HD // 2
@@ -493,23 +514,28 @@
             all_terms[place].extend((first[1][place], second[1][place]))
     encoder = jnp.concatenate(all_terms[3], axis=1)
     for place in range(3):
-        encoder += dot_nt(weights_ref[place], jnp.concatenate(all_terms[place], axis=1).astype(half)).T
+        copies[place].wait()
+        encoder += dot_nt(jnp.concatenate(all_terms[place], axis=1).astype(half), weights_ref[place])
     encoder_ref[...] = encoder * norm
 
 
-def finish(index, sums, weights, norm, own):
-    width = weights.shape[1]
+def finish(index, sums, w_query, w_key, w_value, norm, own):
+    width = w_query.shape[0]
     return pl.pallas_call(
         functools.partial(finish_kernel, norm, own),
         grid_spec=pltpu.PrefetchScalarGridSpec(
             num_scalar_prefetch=1,
             grid=(1,),
-            in_specs=[whole(*sums.shape), whole(*weights.shape)],
+            in_specs=[whole(*sums.shape)] + [pl.BlockSpec(memory_space=pl.ANY)] * 3,
             out_specs=[whole(HD, width)] * 4 + [whole(own, width)],
+            scratch_shapes=[
+                pltpu.VMEM((3, width, width), half),
+                pltpu.SemaphoreType.DMA((3,)),
+            ],
         ),
         out_shape=[jax.ShapeDtypeStruct((HD, width), full)] * 4 + [jax.ShapeDtypeStruct((own, width), full)],
-        compiler_params=pltpu.CompilerParams(vmem_limit_bytes=ROOM),
-    )(index, sums, weights)
+        compiler_params=pltpu.CompilerParams(vmem_limit_bytes=WIDE),
+    )(index, sums, w_query, w_key, w_value)
 
 
 def exchange(array, axis):
@@ -558,19 +584,11 @@
     lanes = [list(range(first, model_size, 2)) for first in range(2)]
     all_cot = lax.all_gather(both, "mp", axis=0, tiled=True, axis_index_groups=lanes)
 
-    pairs = edge_counts(mesh_source, mesh_target, mesh_count, nodes)
     place = model_index.reshape(1).astype(jnp.int32)
-    left, grads = attention(
-        place,
-        encoded,
-        w_encoder,
-        w_query,
-        w_key,
-        w_value,
-        received,
-        pairs,
-        data_size,
+    pairs, folded = edge_counts(
+        mesh_source, mesh_target, mesh_count, place, w_encoder, w_query, w_key, w_value, nodes
     )
+    left, grads = attention(place, encoded, w_encoder, folded, received, pairs, data_size)
 
     shares = exchange(grads, "dp")
     share = jnp.sum(shares.astype(full), axis=0).astype(half)
@@ -581,11 +599,9 @@
     ]
     swapped = lax.ppermute(share, ("dp", "mp"), across)
     met = exchange(meet(left, all_cot, data_size, own_channels), "dp")
-    joined = join(met, swapped, own_channels)
-    weights = bring(w_query, w_key, w_value, joined)
-    sums = exchange(joined, "dp")
+    sums = exchange(join(met, swapped, own_channels), "dp")
     norm = 1.0 / math.sqrt(data_size * nodes)
-    return tuple(finish(place, sums, weights, norm, own_channels))
+    return tuple(finish(place, sums, w_query, w_key, w_value, norm, own_channels))
 
 
 def solution(mesh):

time: 160 us -> 159 us (level)
  blocking collectives: 0 us -> 19.3 us
  local copies, waits for them, and re-layouts: 9.4 us -> 0.8 us
  waiting for transfers between devices: 46.9 us -> 40.3 us
  starting transfers between devices: 41.5 us -> 36.6 us
    all_to_all x0 -> x1, blocking collectives: none -> 19.3 us  [exchange(): return lax.all_to_all(array, axis, split_axis=0, concat_axis=0, tiled=True)]
    all_to_all x5 -> x4, waiting for transfers between devices: 32 us -> 23.1 us  [exchange(): return lax.all_to_all(array, axis, split_axis=0, concat_axis=0, tiled=True)]
    unnamed x16 -> x6, local copies, waits for them, and re-layouts: 9.4 us -> 0.8 us
    all_to_all x5 -> x4, starting transfers between devices: 37.7 us -> 32.6 us  [exchange(): return lax.all_to_all(array, axis, split_axis=0, concat_axis=0, tiled=True)]
    pallas_call x1, Pallas kernels: 2.54 us -> 5.53 us  [finish(): pl.pallas_call(functools.partial(finish_kernel, norm, own), grid_spec=plt...]
    all_gather x1, waiting for transfers between devices: 3.38 us -> 5.97 us  [per_device(): lax.all_gather(both, 'mp', axis=0, tiled=True, axis_index_groups=lanes)]
    pallas_call x1, Pallas kernels: 22.4 us -> 19.8 us  [attention(): pl.pallas_call(attention_kernel, grid_spec=pltpu.PrefetchScalarGridSpec(n...]
  transfers between devices with their start and end apart: 8 -> 7, of which waited for: 8 -> 7; matrix products, arithmetic and copies ran while one was open for 0% -> 0% of each run, Pallas kernels for 22% -> 20%
where the time goes in v4:
time: 159 us; the launch traced here: 158 us
  Pallas kernels  47 us (30%)
  waiting for transfers between devices  40.3 us (25%)
  starting transfers between devices  36.6 us (23%)
  blocking collectives  19.3 us (12%)
  between operations  14.1 us (9%)
    all_to_all x4, starting transfers between devices, exchange(): return lax.all_to_all(array, axis, split_axis=0, concat_axis=0, tiled=True)  32.6 us
    all_to_all x4, waiting for transfers between devices, exchange(): return lax.all_to_all(array, axis, split_axis=0, concat_axis=0, tiled=True)  23.1 us
    pallas_call x1, Pallas kernels, attention(): pl.pallas_call(attention_kernel, grid_spec=pltpu.PrefetchScalarGridSpec(n...  19.8 us
    all_to_all x1, blocking collectives, exchange(): return lax.all_to_all(array, axis, split_axis=0, concat_axis=0, tiled=True)  19.3 us
    pallas_call x1, Pallas kernels, edge_counts(): pl.pallas_call(edges_kernel, grid_spec=pltpu.PrefetchScalarGridSpec(num_s...  9.03 us
    pallas_call x1, Pallas kernels, encoder_partials(): pl.pallas_call(encoder_kernel, grid_spec=pltpu.PrefetchScalarGridSpec(num...  7.94 us
    ppermute x1, waiting for transfers between devices, per_device(): lax.ppermute(local_cot, 'mp', [(i, i ^ 1) for i in range(model_size)])  6.7 us
    all_gather x1, waiting for transfers between devices, per_device(): lax.all_gather(both, 'mp', axis=0, tiled=True, axis_index_groups=lanes)  5.97 us
  transfers between devices with their start and end apart: 7, of which 7 were waited for; matrix products, arithmetic and copies ran while one was open for 0% of the time, Pallas kernels for 20%

profile of v4, /device:TPU:1, one launch (start us, length us, event | category | flops | bytes accessed | tf_op | source)
XLA Modules:
  0.0 158.2 jit_solution(9864397419419252489)
XLA Ops:
  7.2 0.0 copy-start.1
  7.2 7.9 %shard_map.164 = bf16[16,192,128]{2,1,0:T(8,128)(2,1)} custom-call(s32[16]{0:T(128)} %count_ref.2, s32[1]{0:T(128)} %bitcast.2.base_ref, s32[16,2048]{1,0:T(8,128)} %source_ref.2, s32[16,2048]{1,0:T(8,128)} %target_ref.2, bf16[1024,128]{1,0:T(8,128)(2,1)} %bitcast.8, bf16[1024,1024]{1,0:T(8,128)(2,1)} %w_output_ref.1, bf16[128,1024]{1,0:T(8,128)(2,1)} %bitcast.5), custom_call_target="tpu_custom_call" | custom-call | flops 8589934592 | bytes 262144 | tf_op jit(solution)/shard_map/pallas_call | solution.py:90
  15.1 10.1 %all-to-all-start = ((bf16[16,192,128]{2,1,0:T(8,128)(2,1)}), bf16[16,192,128]{2,1,0:T(8,128)(2,1)S(1)}, u32[]{:S(2)}, u32[]{:S(2)}) async-start(bf16[16,192,128]{2,1,0:T(8,128)(2,1)} %shard_map.164), calls=%async_computation | async-start | bytes 1572864 | tf_op jit(solution)/shard_map/all_to_all | solution.py:542
  25.3 0.0 all-gather.2.cloned.1.call-start
  25.3 0.0 copy-done.1
  25.3 1.4 collective-permute-start
  26.8 6.7 %collective-permute-done.other_ref = bf16[128,1024]{1,0:T(8,128)(2,1)S(1)} collective-permute-done((bf16[128,1024]{1,0:T(8,128)(2,1)S(1)}, bf16[128,1024]{1,0:T(8,128)(2,1)S(1)}, u32[]{:S(2)}, u32[]{:S(2)}) %collective-permute-start) | collective-permute-done | bytes 262176 | tf_op jit(solution)/shard_map/ppermute | solution.py:570
  33.5 12.6 %all-to-all-done.received_ref = bf16[16,192,128]{2,1,0:T(8,128)(2,1)S(1)} async-done(((bf16[16,192,128]{2,1,0:T(8,128)(2,1)}), bf16[16,192,128]{2,1,0:T(8,128)(2,1)S(1)}, u32[]{:S(2)}, u32[]{:S(2)}) %all-to-all-start) | async-done | bytes 786464 | tf_op jit(solution)/shard_map/all_to_all | solution.py:542
  46.1 0.0 copy-start
  46.1 1.3 shard_map.165
  47.3 0.0 all-gather.2.cloned.1.call-update
  47.4 5.3 %all-to-all-start.1 = ((bf16[16,128,128]{2,1,0:T(8,128)(2,1)}), bf16[16,128,128]{2,1,0:T(8,128)(2,1)S(1)}, u32[]{:S(2)}, u32[]{:S(2)}) async-start(bf16[16,128,128]{2,1,0:T(8,128)(2,1)} %get-tuple-element.11), calls=%async_computation.1 | async-start | bytes 1048576 | tf_op jit(solution)/shard_map/all_to_all | solution.py:542
  52.6 9.0 %shard_map.166 = (bf16[2048,2048]{1,0:T(8,128)(2,1)}, bf16[256,192]{1,0:T(8,128)(2,1)}) custom-call(s32[16]{0:T(128)} %count_ref.3, s32[1]{0:T(128)} %bitcast.index_ref, s32[16,512]{1,0:T(8,128)} %source_ref.3, s32[16,512]{1,0:T(8,128)} %target_ref.3, bf16[128,1024]{1,0:T(8,128)(2,1)} %w_encoder_ref.3, bf16[1024,1024]{1,0:T(8,128)(2,1)} %w_query_ref.3, ...), custom_call_target="tpu_custom_call" | custom-call | flops 8589934592 | bytes 8388608 | tf_op jit(solution)/shard_map/pallas_call | solution.py:209
  61.7 0.0 copy-done
  61.7 8.4 %all-to-all-done.1.encoded_ref = bf16[16,128,128]{2,1,0:T(8,128)(2,1)S(1)} async-done(((bf16[16,128,128]{2,1,0:T(8,128)(2,1)}), bf16[16,128,128]{2,1,0:T(8,128)(2,1)S(1)}, u32[]{:S(2)}, u32[]{:S(2)}) %all-to-all-start.1) | async-done | bytes 524320 | tf_op jit(solution)/shard_map/all_to_all | solution.py:542
  70.0 0.0 copy-start.2
  70.1 0.8 copy-done.2
  70.8 19.8 %shard_map.167 = (bf16[80,2048]{1,0:T(8,128)(2,1)}, bf16[16,112,128]{2,1,0:T(8,128)(2,1)}) custom-call(s32[1]{0:T(128)} %bitcast.index_ref, bf16[16,128,128]{2,1,0:T(8,128)(2,1)} %copy-done.2, bf16[128,1024]{1,0:T(8,128)(2,1)} %w_encoder_ref.3, bf16[256,192]{1,0:T(8,128)(2,1)} %get-tuple-element.12.folded_ref, bf16[16,192,128]{2,1,0:T(8,128)(2,1)} %copy-done, ...), custom_call_target="tpu_custom_call" | custom-call | flops 3221225472 | bytes 8388608 | tf_op jit(solution)/shard_map/pallas_call | solution.py:351
  90.7 11.2 %all-to-all-start.3 = ((bf16[16,112,128]{2,1,0:T(8,128)(2,1)}), bf16[16,112,128]{2,1,0:T(8,128)(2,1)S(1)}, u32[]{:S(2)}, u32[]{:S(2)}) async-start(bf16[16,112,128]{2,1,0:T(8,128)(2,1)} %get-tuple-element.16), calls=%async_computation.3 | async-start | bytes 917504 | tf_op jit(solution)/shard_map/all_to_all | solution.py:542
  101.8 6.0 %all-gather.2.cloned.1.call-done.cot_ref = bf16[2048,1024]{1,0:T(8,128)(2,1)} async-done(((bf16[256,1024]{1,0:T(8,128)(2,1)}), bf16[2048,1024]{1,0:T(8,128)(2,1)}) %all-gather.2.cloned.1.call-update) | async-done | bytes 4194320 | tf_op jit(solution)/shard_map/all_gather | solution.py:585
  107.8 3.4 %shard_map.168 = bf16[16,48,128]{2,1,0:T(8,128)(2,1)} custom-call(bf16[80,2048]{1,0:T(8,128)(2,1)} %get-tuple-element.14.left_any, bf16[2048,1024]{1,0:T(8,128)(2,1)} %all-gather.2.cloned.1.call-done.cot_ref), custom_call_target="tpu_custom_call" | custom-call | flops 335544320 | bytes 4194304 | tf_op jit(solution)/shard_map/pallas_call | solution.py:426
  111.2 1.1 all-to-all-done.3
  112.3 6.0 %all-to-all-start.2 = ((bf16[16,48,128]{2,1,0:T(8,128)(2,1)}), bf16[16,48,128]{2,1,0:T(8,128)(2,1)S(1)}, u32[]{:S(2)}, u32[]{:S(2)}) async-start(bf16[16,48,128]{2,1,0:T(8,128)(2,1)} %shard_map.168), calls=%async_computation.2 | async-start | bytes 393216 | tf_op jit(solution)/shard_map/all_to_all | solution.py:542
  118.3 0.1 reduce_sum.12
  118.4 2.5 %collective-permute-start.1 = (bf16[112,128]{1,0:T(8,128)(2,1)S(1)}, bf16[112,128]{1,0:T(8,128)(2,1)S(1)}, u32[]{:S(2)}, u32[]{:S(2)}) collective-permute-start(bf16[112,128]{1,0:T(8,128)(2,1)S(1)} %reduce_sum.12), channel_id=1, source_target_pairs={{0,0},{1,1},{2,2},{3,3},{4,4},{5,5},{6,6},{7,7},{8,8},{9,9},{10,10... | collective-permute-start | bytes 86024 | tf_op jit(solution)/shard_map/ppermute | solution.py:600
  120.8 4.5 %collective-permute-done.1.swapped_ref = bf16[112,128]{1,0:T(8,128)(2,1)S(1)} collective-permute-done((bf16[112,128]{1,0:T(8,128)(2,1)S(1)}, bf16[112,128]{1,0:T(8,128)(2,1)S(1)}, u32[]{:S(2)}, u32[]{:S(2)}) %collective-permute-start.1) | collective-permute-done | bytes 28704 | tf_op jit(solution)/shard_map/ppermute | solution.py:600
  125.4 1.1 all-to-all-done.2.met_ref
  126.4 0.1 shard_map.169
  126.5 19.3 %all_to_all.25.sums_ref = bf16[16,144,128]{2,1,0:T(8,128)(2,1)} all-to-all(bf16[16,144,128]{2,1,0:T(8,128)(2,1)S(1)} %shard_map.169), channel_id=1, replica_groups=mesh['dp'=16,'mp'=16] {'dp'}, dimensions={0} | all-to-all | bytes 1179648 | tf_op jit(solution)/shard_map/all_to_all | solution.py:542
  145.8 5.5 %shard_map.170 = (f32[64,1024]{1,0:T(8,128)}, f32[64,1024]{1,0:T(8,128)}, f32[64,1024]{1,0:T(8,128)}, f32[64,1024]{1,0:T(8,128)}, f32[8,1024]{1,0:T(8,128)}) custom-call(s32[1]{0:T(128)} %bitcast.index_ref, bf16[16,144,128]{2,1,0:T(8,128)(2,1)} %all_to_all.25.sums_ref, bf16[1024,1024]{1,0:T(8,128)(2,1)} %w_query_ref.3, bf16[1024,1024]{1,0:T(8,128)(2,1)} %w_key_ref.3, ...), custom_call_target="tpu_custom_call" | custom-call | tf_op jit(solution)/shard_map/pallas_call | solution.py:524
Async XLA Ops:
  7.2 18.2 %copy-start.1 = (bf16[1,128,1024]{2,1,0:T(8,128)(2,1)S(1)}, bf16[1,128,1024]{2,1,0:T(8,128)(2,1)}, u32[]{:S(2)}) copy-start(bf16[1,128,1024]{2,1,0:T(8,128)(2,1)} %param.14) | copy-start | bytes 786436
  15.1 30.9 %all-to-all-start = ((bf16[16,192,128]{2,1,0:T(8,128)(2,1)}), bf16[16,192,128]{2,1,0:T(8,128)(2,1)S(1)}, u32[]{:S(2)}, u32[]{:S(2)}) async-start(bf16[16,192,128]{2,1,0:T(8,128)(2,1)} %shard_map.164), calls=%async_computation | async-start | bytes 1572864 | tf_op jit(solution)/shard_map/all_to_all | solution.py:542
  25.3 82.5 %all-gather.2.cloned.1.call-start = ((), (), s32[]{:S(2)}) async-start(), calls=%async_computation.5 | async-start | bytes 4718592 | tf_op jit(solution)/shard_map/all_gather | solution.py:585
  25.3 8.1 %collective-permute-start = (bf16[128,1024]{1,0:T(8,128)(2,1)S(1)}, bf16[128,1024]{1,0:T(8,128)(2,1)S(1)}, u32[]{:S(2)}, u32[]{:S(2)}) collective-permute-start(bf16[128,1024]{1,0:T(8,128)(2,1)S(1)} %bitcast.6), channel_id=1, source_target_pairs={{0,1},{1,0},{2,3},{3,2},{4,5},{5,4},{6,7},{7,6},{8,9},{9,8},{10,11... | collective-permute-start | bytes 786440 | tf_op jit(solution)/shard_map/ppermute | solution.py:570
  46.1 15.6 %copy-start = (bf16[16,192,128]{2,1,0:T(8,128)(2,1)}, bf16[16,192,128]{2,1,0:T(8,128)(2,1)S(1)}, u32[]{:S(2)}) copy-start(bf16[16,192,128]{2,1,0:T(8,128)(2,1)S(1)} %all-to-all-done.received_ref) | copy-start | bytes 2359300
  47.4 22.7 %all-to-all-start.1 = ((bf16[16,128,128]{2,1,0:T(8,128)(2,1)}), bf16[16,128,128]{2,1,0:T(8,128)(2,1)S(1)}, u32[]{:S(2)}, u32[]{:S(2)}) async-start(bf16[16,128,128]{2,1,0:T(8,128)(2,1)} %get-tuple-element.11), calls=%async_computation.1 | async-start | bytes 1048576 | tf_op jit(solution)/shard_map/all_to_all | solution.py:542
  70.0 0.8 copy-start.2
  90.7 21.6 %all-to-all-start.3 = ((bf16[16,112,128]{2,1,0:T(8,128)(2,1)}), bf16[16,112,128]{2,1,0:T(8,128)(2,1)S(1)}, u32[]{:S(2)}, u32[]{:S(2)}) async-start(bf16[16,112,128]{2,1,0:T(8,128)(2,1)} %get-tuple-element.16), calls=%async_computation.3 | async-start | bytes 917504 | tf_op jit(solution)/shard_map/all_to_all | solution.py:542
  112.3 14.2 %all-to-all-start.2 = ((bf16[16,48,128]{2,1,0:T(8,128)(2,1)}), bf16[16,48,128]{2,1,0:T(8,128)(2,1)S(1)}, u32[]{:S(2)}, u32[]{:S(2)}) async-start(bf16[16,48,128]{2,1,0:T(8,128)(2,1)} %shard_map.168), calls=%async_computation.2 | async-start | bytes 393216 | tf_op jit(solution)/shard_map/all_to_all | solution.py:542
  118.4 7.0 %collective-permute-start.1 = (bf16[112,128]{1,0:T(8,128)(2,1)S(1)}, bf16[112,128]{1,0:T(8,128)(2,1)S(1)}, u32[]{:S(2)}, u32[]{:S(2)}) collective-permute-start(bf16[112,128]{1,0:T(8,128)(2,1)S(1)} %reduce_sum.12), channel_id=1, source_target_pairs={{0,0},{1,1},{2,2},{3,3},{4,4},{5,5},{6,6},{7,7},{8,8},{9,9},{10,10... | collective-permute-start | bytes 86024 | tf_op jit(solution)/shard_map/ppermute | solution.py:600
Sparse Core Ops, SparseCore 0:
  47.5 60.2 all-gather.1

commit v5 on v4

--- a/solution.py
+++ b/solution.py
@@ -114,14 +114,30 @@
     )(count, base, source, target, local_grid, w_output, local_cot)
 
 
-def collect_kernel(odd_ref, received_ref, own_ref, other_ref, copies_ref, both_ref):
+def collect_kernel(received_ref, copies_ref):
     parts, rows, _ = copies_ref.shape
-    total = received_ref[0, :rows, :].astype(full)
+    total = received_ref[0].astype(full)
     for part in range(1, parts):
-        total += received_ref[part, :rows, :].astype(full)
+        total += received_ref[part].astype(full)
     total = total.astype(half)
     for part in range(parts):
         copies_ref[part] = total
+
+
+def collect(received, rows):
+    parts, _, channels = received.shape
+    return pl.pallas_call(
+        collect_kernel,
+        grid=(1,),
+        in_specs=[whole(parts, rows, channels)],
+        out_specs=whole(parts, rows, channels),
+        out_shape=jax.ShapeDtypeStruct((parts, rows, channels), half),
+        compiler_params=pltpu.CompilerParams(vmem_limit_bytes=SMALL),
+    )(received)
+
+
+def pair_kernel(odd_ref, own_ref, other_ref, both_ref):
+    rows = own_ref.shape[0]
     own, other = own_ref[...], other_ref[...]
     odd = odd_ref[0] == 1
 
@@ -136,23 +152,19 @@
         both_ref[rows:, :] = other
 
 
-def collect(odd, received, own, other):
-    parts, _, channels = received.shape
+def pair_up(odd, own, other):
     rows, width = own.shape
     return pl.pallas_call(
-        collect_kernel,
+        pair_kernel,
         grid_spec=pltpu.PrefetchScalarGridSpec(
             num_scalar_prefetch=1,
             grid=(1,),
-            in_specs=[whole(*received.shape), whole(rows, width), whole(rows, width)],
-            out_specs=[whole(parts, rows, channels), whole(2 * rows, width)],
-        ),
-        out_shape=[
-            jax.ShapeDtypeStruct((parts, rows, channels), half),
-            jax.ShapeDtypeStruct((2 * rows, width), half),
-        ],
+            in_specs=[whole(rows, width), whole(rows, width)],
+            out_specs=whole(2 * rows, width),
+        ),
+        out_shape=jax.ShapeDtypeStruct((2 * rows, width), half),
         compiler_params=pltpu.CompilerParams(vmem_limit_bytes=SMALL),
-    )(odd, received, own, other)
+    )(odd, own, other)
 
 
 def split(value):
@@ -460,8 +472,7 @@
         out_ref[part] = joined
 
 
-def join(met, swapped, own):
-    parts = met.shape[0]
+def join(met, swapped, own, parts):
     rows, columns = swapped.shape
     return pl.pallas_call(
         functools.partial(join_kernel, own),
@@ -578,28 +589,33 @@
         w_output,
         local_cot,
     )
+    partials, mesh_count = lax.optimization_barrier((partials, mesh_count))
     received = exchange(partials, "mp")
-    copies, both = collect((model_index % 2).reshape(1).astype(jnp.int32), received, local_cot, other)
+    copies = collect(received, node_rows)
     encoded = exchange(copies, "mp")
-    lanes = [list(range(first, model_size, 2)) for first in range(2)]
-    all_cot = lax.all_gather(both, "mp", axis=0, tiled=True, axis_index_groups=lanes)
-
     place = model_index.reshape(1).astype(jnp.int32)
     pairs, folded = edge_counts(
         mesh_source, mesh_target, mesh_count, place, w_encoder, w_query, w_key, w_value, nodes
     )
+    pairs, other = lax.optimization_barrier((pairs, other))
+    both = pair_up((model_index % 2).reshape(1).astype(jnp.int32), local_cot, other)
+    lanes = [list(range(first, model_size, 2)) for first in range(2)]
+    all_cot = lax.all_gather(both, "mp", axis=0, tiled=True, axis_index_groups=lanes)
     left, grads = attention(place, encoded, w_encoder, folded, received, pairs, data_size)
 
-    shares = exchange(grads, "dp")
+    packed = jnp.concatenate([grads, meet(left, all_cot, data_size, own_channels)], axis=1)
+    shares = exchange(packed, "dp")
     share = jnp.sum(shares.astype(full), axis=0).astype(half)
+    rows = grads.shape[1]
+    met = share[None, rows:]
+    share = share[:rows]
     across = [
         (data * model_size + model, data * model_size + (model + data) % model_size)
         for data in range(data_size)
         for model in range(model_size)
     ]
     swapped = lax.ppermute(share, ("dp", "mp"), across)
-    met = exchange(meet(left, all_cot, data_size, own_channels), "dp")
-    sums = exchange(join(met, swapped, own_channels), "dp")
+    sums = exchange(join(met, swapped, own_channels, data_size), "dp")
     norm = 1.0 / math.sqrt(data_size * nodes)
     return tuple(finish(place, sums, w_query, w_key, w_value, norm, own_channels))
 

time: 159 us -> 174 us (1.094)
  blocking collectives: 19.3 us -> 101 us
  waiting for transfers between devices: 40.3 us -> 5.99 us
  starting transfers between devices: 36.6 us -> 4.17 us
    all_to_all x1 -> x4, blocking collectives: 19.3 us -> 101 us  [exchange(): return lax.all_to_all(array, axis, split_axis=0, concat_axis=0, tiled=True)]
    all_to_all x4 -> x0, starting transfers between devices: 32.6 us -> none  [exchange(): return lax.all_to_all(array, axis, split_axis=0, concat_axis=0, tiled=True)]
    all_to_all x4 -> x0, waiting for transfers between devices: 23.1 us -> none  [exchange(): return lax.all_to_all(array, axis, split_axis=0, concat_axis=0, tiled=True)]
    ppermute x1, waiting for transfers between devices: 6.7 us -> 0.01 us  [per_device(): lax.ppermute(local_cot, 'mp', [(i, i ^ 1) for i in range(model_size)])]
    all_gather x1, waiting for transfers between devices: 5.97 us -> 1.18 us  [per_device(): lax.all_gather(both, 'mp', axis=0, tiled=True, axis_index_groups=lanes)]
  transfers between devices with their start and end apart: 7 -> 3, of which waited for: 7 -> 2; matrix products, arithmetic and copies ran while one was open for 0% -> 0% of each run, Pallas kernels for 20% -> 21%
where the time goes in v5:
time: 174 us
  blocking collectives  101 us (58%)
  Pallas kernels  46.8 us (27%)
  between operations  14.1 us (8%)
  waiting for transfers between devices  5.99 us (3%)
  starting transfers between devices  4.17 us (2%)
    all_to_all x4, blocking collectives, exchange(): return lax.all_to_all(array, axis, split_axis=0, concat_axis=0, tiled=True)  101 us
    pallas_call x1, Pallas kernels, attention(): pl.pallas_call(attention_kernel, grid_spec=pltpu.PrefetchScalarGridSpec(n...  19.8 us
    pallas_call x1, Pallas kernels, edge_counts(): pl.pallas_call(edges_kernel, grid_spec=pltpu.PrefetchScalarGridSpec(num_s...  9.1 us
    pallas_call x1, Pallas kernels, encoder_partials(): pl.pallas_call(encoder_kernel, grid_spec=pltpu.PrefetchScalarGridSpec(num...  7.86 us
    pallas_call x1, Pallas kernels, finish(): pl.pallas_call(functools.partial(finish_kernel, norm, own), grid_spec=plt...  5.53 us
    ppermute x1, waiting for transfers between devices, per_device(): swapped = lax.ppermute(share, ('dp', 'mp'), across)  4.78 us
  transfers between devices with their start and end apart: 3, of which 2 were waited for; matrix products, arithmetic and copies ran while one was open for 0% of the time, Pallas kernels for 21%

profile of v5, /device:TPU:1, one launch (start us, length us, event | category | flops | bytes accessed | tf_op | source)
XLA Modules:
  0.0 174.0 jit_solution(13025204801538277929)
XLA Ops:
  7.2 0.0 all-gather.2.cloned.1.call-start
  7.2 2.2 %collective-permute-start = (bf16[128,1024]{1,0:T(8,128)(2,1)}, bf16[128,1024]{1,0:T(8,128)(2,1)S(1)}, u32[]{:S(2)}, u32[]{:S(2)}) collective-permute-start(bf16[128,1024]{1,0:T(8,128)(2,1)} %bitcast.7), channel_id=1, source_target_pairs={{0,1},{1,0},{2,3},{3,2},{4,5},{5,4},{6,7},{7,6},{8,9},{9,8},{10,11... | collective-permute-start | bytes 786440 | tf_op jit(solution)/shard_map/ppermute | solution.py:581
  9.4 7.9 %shard_map.164 = bf16[16,192,128]{2,1,0:T(8,128)(2,1)} custom-call(s32[16]{0:T(128)} %count_ref.1, s32[1]{0:T(128)} %bitcast.1.base_ref, s32[16,2048]{1,0:T(8,128)} %source_ref.2, s32[16,2048]{1,0:T(8,128)} %target_ref.2, bf16[1024,128]{1,0:T(8,128)(2,1)} %bitcast.10, bf16[1024,1024]{1,0:T(8,128)(2,1)} %w_output_ref.1, bf16[128,1024]{1,0:T(8,128)(2,1)} %bitcast.8), custom_call_target="tpu_custom_call" | custom-call | flops 8589934592 | bytes 262144 | tf_op jit(solution)/shard_map/pallas_call | solution.py:90
  17.3 0.0 copy-start.1
  17.3 9.1 %shard_map.166 = (bf16[2048,2048]{1,0:T(8,128)(2,1)}, bf16[256,192]{1,0:T(8,128)(2,1)}) custom-call(s32[16]{0:T(128)} %count_ref.2, s32[1]{0:T(128)} %bitcast.index_ref, s32[16,512]{1,0:T(8,128)} %source_ref.3, s32[16,512]{1,0:T(8,128)} %target_ref.3, bf16[128,1024]{1,0:T(8,128)(2,1)} %w_encoder_ref.3, bf16[1024,1024]{1,0:T(8,128)(2,1)} %w_query_ref.3, ...), custom_call_target="tpu_custom_call" | custom-call | flops 8589934592 | bytes 8388608 | tf_op jit(solution)/shard_map/pallas_call | solution.py:221
  26.4 0.0 copy-start.2
  26.4 0.0 collective-permute-done.other_ref
  26.4 0.0 copy-done.1
  26.4 0.8 shard_map.168
  27.3 0.0 all-gather.2.cloned.1.call-update
  27.3 0.4 copy-done.2
  27.7 34.6 %all_to_all.20.received_ref = bf16[16,192,128]{2,1,0:T(8,128)(2,1)S(1)} all-to-all(bf16[16,192,128]{2,1,0:T(8,128)(2,1)S(1)} %copy-done.2), channel_id=1, replica_groups=mesh['dp'=16,'mp'=16] {'mp'}, dimensions={0} | all-to-all | bytes 1572864 | tf_op jit(solution)/shard_map/all_to_all | solution.py:553
  62.4 0.0 copy-start
  62.4 0.1 shard_map.165
  62.5 24.3 %all_to_all.21.encoded_ref = bf16[16,128,128]{2,1,0:T(8,128)(2,1)} all-to-all(bf16[16,128,128]{2,1,0:T(8,128)(2,1)S(1)} %shard_map.165), channel_id=1, replica_groups=mesh['dp'=16,'mp'=16] {'mp'}, dimensions={0} | all-to-all | bytes 1048576 | tf_op jit(solution)/shard_map/all_to_all | solution.py:553
  86.8 0.0 copy-done
  86.8 19.8 %shard_map.167 = (bf16[80,2048]{1,0:T(8,128)(2,1)}, bf16[16,112,128]{2,1,0:T(8,128)(2,1)}) custom-call(s32[1]{0:T(128)} %bitcast.index_ref, bf16[16,128,128]{2,1,0:T(8,128)(2,1)} %all_to_all.21.encoded_ref, bf16[128,1024]{1,0:T(8,128)(2,1)} %w_encoder_ref.3, bf16[256,192]{1,0:T(8,128)(2,1)} %get-tuple-element.15.folded_ref, bf16[16,192,128]{2,1,0:T(8,128)(2,1)} %copy-done, ...), custom_call_target="tpu_custom_call" | custom-call | flops 3221225472 | bytes 8388608 | tf_op jit(solution)/shard_map/pallas_call | solution.py:363
  106.6 1.2 all-gather.2.cloned.1.call-done.cot_ref
  107.8 0.0 copy-start.3
  107.8 3.4 %shard_map.169 = bf16[16,48,128]{2,1,0:T(8,128)(2,1)} custom-call(bf16[80,2048]{1,0:T(8,128)(2,1)} %get-tuple-element.19.left_any, bf16[2048,1024]{1,0:T(8,128)(2,1)} %all-gather.2.cloned.1.call-done.cot_ref), custom_call_target="tpu_custom_call" | custom-call | flops 335544320 | bytes 4194304 | tf_op jit(solution)/shard_map/pallas_call | solution.py:438
  111.2 0.0 copy-done.3
  111.3 1.0 pad_maximum_fusion
  112.2 23.8 %all_to_all.22 = bf16[16,160,128]{2,1,0:T(8,128)(2,1)S(1)} all-to-all(bf16[16,160,128]{2,1,0:T(8,128)(2,1)S(1)} %pad_maximum_fusion), channel_id=1, replica_groups=mesh['dp'=16,'mp'=16] {'dp'}, dimensions={0} | all-to-all | bytes 1310720 | tf_op jit(solution)/shard_map/all_to_all | solution.py:553
  136.0 0.1 reduce_sum.12
  136.1 1.9 %collective-permute-start.1 = (bf16[112,128]{1,0:T(8,128)(2,1)S(1)}, bf16[112,128]{1,0:T(8,128)(2,1)S(1)}, u32[]{:S(2)}, u32[]{:S(2)}) collective-permute-start(bf16[112,128]{1,0:T(8,128)(2,1)S(1)} %slice.9), channel_id=1, source_target_pairs={{0,0},{1,1},{2,2},{3,3},{4,4},{5,5},{6,6},{7,7},{8,8},{9,9},{10,10... | collective-permute-start | bytes 86024 | tf_op jit(solution)/shard_map/ppermute | solution.py:617
  138.1 4.8 %collective-permute-done.1.swapped_ref = bf16[112,128]{1,0:T(8,128)(2,1)S(1)} collective-permute-done((bf16[112,128]{1,0:T(8,128)(2,1)S(1)}, bf16[112,128]{1,0:T(8,128)(2,1)S(1)}, u32[]{:S(2)}, u32[]{:S(2)}) %collective-permute-start.1) | collective-permute-done | bytes 28704 | tf_op jit(solution)/shard_map/ppermute | solution.py:617
  142.8 0.1 shard_map.170
  142.9 18.7 %all_to_all.23.sums_ref = bf16[16,144,128]{2,1,0:T(8,128)(2,1)} all-to-all(bf16[16,144,128]{2,1,0:T(8,128)(2,1)S(1)} %shard_map.170), channel_id=1, replica_groups=mesh['dp'=16,'mp'=16] {'dp'}, dimensions={0} | all-to-all | bytes 1179648 | tf_op jit(solution)/shard_map/all_to_all | solution.py:553
  161.6 5.5 %shard_map.171 = (f32[64,1024]{1,0:T(8,128)}, f32[64,1024]{1,0:T(8,128)}, f32[64,1024]{1,0:T(8,128)}, f32[64,1024]{1,0:T(8,128)}, f32[8,1024]{1,0:T(8,128)}) custom-call(s32[1]{0:T(128)} %bitcast.index_ref, bf16[16,144,128]{2,1,0:T(8,128)(2,1)} %all_to_all.23.sums_ref, bf16[1024,1024]{1,0:T(8,128)(2,1)} %w_query_ref.3, bf16[1024,1024]{1,0:T(8,128)(2,1)} %w_key_ref.3, ...), custom_call_target="tpu_custom_call" | custom-call | tf_op jit(solution)/shard_map/pallas_call | solution.py:535
  (2 shorter events, 0.0 us)
Async XLA Ops:
  7.2 100.7 %all-gather.2.cloned.1.call-start = ((), (), s32[]{:S(2)}) async-start(), calls=%async_computation.4 | async-start | bytes 4718592 | tf_op jit(solution)/shard_map/all_gather | solution.py:603
  7.2 19.2 %collective-permute-start = (bf16[128,1024]{1,0:T(8,128)(2,1)}, bf16[128,1024]{1,0:T(8,128)(2,1)S(1)}, u32[]{:S(2)}, u32[]{:S(2)}) collective-permute-start(bf16[128,1024]{1,0:T(8,128)(2,1)} %bitcast.7), channel_id=1, source_target_pairs={{0,1},{1,0},{2,3},{3,2},{4,5},{5,4},{6,7},{7,6},{8,9},{9,8},{10,11... | collective-permute-start | bytes 786440 | tf_op jit(solution)/shard_map/ppermute | solution.py:581
  17.3 9.1 %copy-start.1 = (bf16[1,128,1024]{2,1,0:T(8,128)(2,1)S(1)}, bf16[1,128,1024]{2,1,0:T(8,128)(2,1)}, u32[]{:S(2)}) copy-start(bf16[1,128,1024]{2,1,0:T(8,128)(2,1)} %param.14) | copy-start | bytes 786436
  26.4 1.3 copy-start.2
  62.4 24.4 %copy-start = (bf16[16,192,128]{2,1,0:T(8,128)(2,1)}, bf16[16,192,128]{2,1,0:T(8,128)(2,1)S(1)}, u32[]{:S(2)}) copy-start(bf16[16,192,128]{2,1,0:T(8,128)(2,1)S(1)} %all_to_all.20.received_ref) | copy-start | bytes 2359300
  107.8 3.4 %copy-start.3 = (bf16[16,112,128]{2,1,0:T(8,128)(2,1)S(1)}, bf16[16,112,128]{2,1,0:T(8,128)(2,1)}, u32[]{:S(2)}) copy-start(bf16[16,112,128]{2,1,0:T(8,128)(2,1)} %get-tuple-element.18) | copy-start | bytes 1376260
  136.1 6.7 %collective-permute-start.1 = (bf16[112,128]{1,0:T(8,128)(2,1)S(1)}, bf16[112,128]{1,0:T(8,128)(2,1)S(1)}, u32[]{:S(2)}, u32[]{:S(2)}) collective-permute-start(bf16[112,128]{1,0:T(8,128)(2,1)S(1)} %slice.9), channel_id=1, source_target_pairs={{0,0},{1,1},{2,2},{3,3},{4,4},{5,5},{6,6},{7,7},{8,8},{9,9},{10,10... | collective-permute-start | bytes 86024 | tf_op jit(solution)/shard_map/ppermute | solution.py:617
Sparse Core Ops, SparseCore 0:
  27.4 80.3 all-gather.1
